TPU v7x, 256 devices: a whole 4x4x8 slice. The times are simulated.
256 devices in a mesh: dp: 32 (over y, z), tensor: 8 (over x, core).
Axes of the slice: x: 4, y: 4, z: 8, core: 2. Of those that a mesh axis runs over, the one named last changes fastest.
Arguments:
- inputs: bfloat16 [4096, 1152], P('dp'), may hold values from -20 to 20
- gate_weight: bfloat16 [1152, 6912], P(None, 'tensor'), may hold values from -0.1875 to 0.1875
- up_weight: bfloat16 [1152, 6912], P(None, 'tensor'), may hold values from -1 to 1
- down_weight: bfloat16 [1152, 6912], P(None, 'tensor'), may hold values from -1 to 1
- out_grad: bfloat16 [4096, 1152], P('dp'), may hold values from -1 to 1
- later_norms: float32 [32], P('dp'), may hold values from 0.1 to 10
Outputs:
- input_grad: bfloat16 [4096, 1152], P(('dp', 'tensor'))
- gate_grad: float32 [1152, 6912], P('dp', 'tensor')
- up_grad: float32 [1152, 6912], P('dp', 'tensor')
- down_grad: float32 [1152, 6912], P('dp', 'tensor')
All inputs are finite; a program needn't handle non-finite values.
Results may differ from a plain program's by a relative error of at most 0.0049.
Values sent between devices are 32-bit elements; how exact they have to be, the bound alone decides.
No kernel may reach another device: no remote copies, remote signals or barrier semaphores. Data moves between devices by JAX's collectives and lax.ppermute only.
A program may use at most 128 MiB of HBM per device.

v0:
```python
import math

import jax
import jax.numpy as jnp
from jax import lax
from jax.sharding import PartitionSpec as P

CLIP_NORM = 1.8
GELU_C = 0.7978845608028654


def gelu_parts(pre):
    tangent = jnp.tanh(GELU_C * (pre + 0.044715 * pre * pre * pre))
    activated = 0.5 * pre * (1.0 + tangent)
    gelu_slope = 0.5 * (1.0 + tangent) + 0.5 * pre * (1.0 - tangent * tangent) * GELU_C * (
        1.0 + 3.0 * 0.044715 * pre * pre
    )
    return (activated, gelu_slope)


def token_products(left, right):
    return lax.dot_general(
        left, right, (((0,), (0,)), ((), ())), preferred_element_type=jnp.float32
    )


def per_device(inputs, gate_weight, up_weight, down_weight, out_grad, later_norms):
    gate_pre = jnp.dot(inputs, gate_weight, preferred_element_type=jnp.float32)
    up_pre = jnp.dot(inputs, up_weight, preferred_element_type=jnp.float32)
    activated, gelu_slope = gelu_parts(gate_pre)
    hidden = (activated * up_pre).astype(jnp.bfloat16)
    hidden_grad = jnp.dot(out_grad, down_weight, preferred_element_type=jnp.float32)
    gate_back = (hidden_grad * up_pre * gelu_slope).astype(jnp.bfloat16)
    up_back = (hidden_grad * activated).astype(jnp.bfloat16)
    feature_contract = (((1,), (1,)), ((), ()))
    input_grad = lax.psum_scatter(
        lax.dot_general(
            gate_back, gate_weight, feature_contract, preferred_element_type=jnp.float32
        )
        + lax.dot_general(up_back, up_weight, feature_contract, preferred_element_type=jnp.float32),
        "tensor",
        scatter_dimension=0,
        tiled=True,
    ).astype(jnp.bfloat16)
    ex_count = later_norms.shape[0]
    seq_len = inputs.shape[0] // ex_count

    def split_examples(matrix):
        return matrix.reshape(ex_count, seq_len, matrix.shape[1])

    def gram_matrix(matrix):
        pieces = split_examples(matrix)
        return jnp.einsum("esd,etd->est", pieces, pieces, preferred_element_type=jnp.float32)

    input_gram = gram_matrix(inputs)
    own_part = jnp.sum(
        input_gram * (gram_matrix(gate_back) + gram_matrix(up_back))
        + gram_matrix(out_grad) * gram_matrix(hidden),
        axis=(1, 2),
    )
    own_norm = lax.psum(own_part, "tensor")
    width = inputs.shape[1]
    full_hidden = gate_weight.shape[1] * lax.axis_size("tensor")
    examples_all = ex_count * lax.axis_size("dp")
    clip_factor = jnp.minimum(1.0, CLIP_NORM / jnp.sqrt(later_norms + own_norm))
    token_weight = jnp.repeat(clip_factor * math.sqrt(width * full_hidden / examples_all), seq_len)[
        :, None
    ]
    weighted_gate = (gate_back * token_weight).astype(jnp.bfloat16)
    weighted_up = (up_back * token_weight).astype(jnp.bfloat16)
    weighted_hidden = (hidden * token_weight).astype(jnp.bfloat16)
    down_grad = lax.psum_scatter(
        token_products(out_grad, weighted_hidden), "dp", scatter_dimension=0, tiled=True
    )
    gate_grad = lax.psum_scatter(
        token_products(inputs, weighted_gate), "dp", scatter_dimension=0, tiled=True
    )
    up_grad = lax.psum_scatter(
        token_products(inputs, weighted_up), "dp", scatter_dimension=0, tiled=True
    )
    return (input_grad, gate_grad, up_grad, down_grad)


def solution(mesh):
    in_specs = (
        P("dp", None),
        P(None, "tensor"),
        P(None, "tensor"),
        P(None, "tensor"),
        P("dp", None),
        P("dp"),
    )
    out_specs = (P(("dp", "tensor"), None), P("dp", "tensor"), P("dp", "tensor"), P("dp", "tensor"))
    return jax.shard_map(
        per_device, mesh=mesh, in_specs=in_specs, out_specs=out_specs, check_vma=False
    )
```

profile of v0, /device:TPU:96, one launch (start us, length us, event | category | flops | bytes accessed | tf_op | source)
XLA Modules:
  0.0 313.0 jit_solution(14670764836576091218)
XLA Ops:
  8.0 0.0 copy-start
  8.0 0.0 copy-start.3
  8.0 0.0 reduce-scatter.5.cloned.1.call-start
  8.1 0.0 copy-start.4
  8.1 2.5 fusion.14
  10.6 0.0 copy-done.3
  10.6 0.0 copy-done.4
  10.6 0.0 copy-start.2
  10.6 0.7 fusion.13
  11.3 0.0 copy-done
  11.3 0.3 copy-done.2
  11.6 0.0 copy-start.1
  11.6 0.9 multiply_convert_fusion.3
  12.6 0.6 copy-done.1
  13.2 0.5 fusion.15
  13.7 1.4 convolution_add_fusion
  15.1 0.0 reduce-scatter.5.cloned.1.call-update
  15.1 0.0 all-reduce.6.cloned.1.call-start
  15.2 0.2 fusion.16
  15.4 0.3 fusion.17
  15.7 0.2 fusion.18
  15.9 0.3 fusion.1
  16.2 0.9 fusion.2
  17.0 15.2 %psum.7 = f32[1]{0:T(128)} all-reduce(f32[1]{0:T(128)} %bitcast), channel_id=1, replica_groups=mesh['dp'=32,'tensor'=8] {'tensor'}, use_global_device_ids=true, to_apply=%region_2.0 | all-reduce | flops 1 | bytes 8 | tf_op jit(solution)/shard_map/psum | solution.py:61
  33.6 2.6 convolution_bitcast_fusion.2
  36.2 2.6 convolution_bitcast_fusion.1
  38.8 2.6 convolution_bitcast_fusion
  41.4 0.0 copy-start.5
  41.4 0.0 all-reduce.6.cloned.1.call-update
  41.5 0.6 copy-done.5
  42.1 0.6 dynamic-slice
  43.3 7.4 %reduce-scatter.5.cloned.1.call-done = f32[16,1152]{1,0:T(8,128)} async-done(((f32[128,1152]{1,0:T(8,128)}), f32[16,1152]{1,0:T(8,128)}) %reduce-scatter.5.cloned.1.call-update) | async-done | bytes 73744 | tf_op jit(solution)/shard_map/reduce_scatter | solution.py:36
  50.7 1.5 convert_element_type.32
  52.2 247.7 %all-reduce.6.cloned.1.call-done = (f32[1152,864]{0,1:T(8,128)}, f32[1152,864]{0,1:T(8,128)}, f32[1152,864]{0,1:T(8,128)}) async-done(((f32[1152,864]{0,1:T(8,128)}, f32[1152,864]{0,1:T(8,128)}, f32[1152,864]{0,1:T(8,128)}), (f32[1152,864]{0,1:T(8,128)}, f32[1152,864]{0,1:T(8,128)}, f32[1152,864]{0,1:T(8,128)})) %all-reduce.6.cloned.1.call-update) | async-done | bytes 11943952
  299.9 1.3 constant_dynamic-slice_fusion.2
  301.2 0.9 copy.13
  302.1 1.7 constant_dynamic-slice_fusion
  303.8 0.9 copy.14
  304.7 0.8 copy.15
Async XLA Ops:
  8.0 3.3 %copy-start = (bf16[1152,864]{0,1:T(8,128)(2,1)S(1)}, bf16[1152,864]{0,1:T(8,128)(2,1)}, u32[]{:S(2)}) copy-start(bf16[1152,864]{0,1:T(8,128)(2,1)} %param.8) | copy-start | bytes 5971972
  8.0 2.5 copy-start.3
  8.0 42.7 %reduce-scatter.5.cloned.1.call-start = ((), (), s32[]{:S(2)}) async-start(), calls=%async_computation.1 | async-start | bytes 663552 | tf_op jit(solution)/shard_map/reduce_scatter | solution.py:36
  8.1 2.5 copy-start.4
  10.6 1.1 copy-start.2
  11.6 1.6 copy-start.1
  15.1 284.8 %all-reduce.6.cloned.1.call-start = ((), (), s32[]{:S(2)}) async-start(), calls=%async_computation.2 | async-start | bytes 23887872
  41.4 0.7 copy-start.5
Sparse Core Ops, SparseCore 0:
  15.2 35.4 reduce-scatter.4
Sparse Core Ops, SparseCore 1:
  41.5 258.3 all-reduce.5
where the time goes:
time: 315 us; the launch traced here: 313 us
  waiting for transfers between devices  255 us (81%)
  between operations  17.6 us (6%)
  matrix products  15.6 us (5%)
  blocking collectives  15.2 us (5%)
  local copies, waits for them, and re-layouts  7.86 us (2%)
    unnamed x3, waiting for transfers between devices  248 us
    psum x1, blocking collectives, per_device(): own_norm = lax.psum(own_part, 'tensor')  15.2 us
    unnamed x18, local copies, waits for them, and re-layouts  7.86 us
    dot_general x3, matrix products, token_products(): lax.dot_general(left, right, (((0,), (0,)), ((), ())), preferred_element_...  7.83 us
    reduce_scatter x1, waiting for transfers between devices, per_device(): lax.psum_scatter(lax.dot_general(gate_back, gate_weight, feature_contract...  7.37 us
  transfers between devices with their start and end apart: 2, of which 2 were waited for; matrix products, arithmetic and copies ran while one was open for 4% of the time, Pallas kernels for 0%

commit v1 on v0

v1 whole, which is shorter than its diff:
```python
import math

import jax
import jax.numpy as jnp
from jax import lax
from jax.experimental import pallas as pl
from jax.experimental.pallas import tpu as pltpu
from jax.sharding import Mesh, PartitionSpec as P

CLIP_NORM = 1.8
GELU_C = 0.7978845608028654
NY, NZ, NX, NC = 4, 8, 4, 2
VMEM_LIMIT = 48 * 1024 * 1024
F32 = jnp.float32
BF16 = jnp.bfloat16


def gelu_parts(pre):
    tangent = jnp.tanh(GELU_C * (pre + 0.044715 * pre * pre * pre))
    activated = 0.5 * pre * (1.0 + tangent)
    gelu_slope = 0.5 * (1.0 + tangent) + 0.5 * pre * (1.0 - tangent * tangent) * GELU_C * (
        1.0 + 3.0 * 0.044715 * pre * pre
    )
    return (activated, gelu_slope)


def shift(array, axis, step):
    size = lax.axis_size(axis)
    return lax.ppermute(array, axis, [(i, (i + step) % size) for i in range(size)])


def dot(left, right, dims):
    return lax.dot_general(left, right, (dims, ((), ())), preferred_element_type=F32)


def own_kernel(x_ref, dy_ref, wg_ref, wu_ref, wd_ref, g_ref, u_ref, h_ref, own_ref):
    x = x_ref[...]
    dy = dy_ref[...]
    g, u, h = forward(x, dy, wg_ref[...], wu_ref[...], wd_ref[...])
    g_ref[...] = g
    u_ref[...] = u
    h_ref[...] = h
    own = jnp.sum(gram(x) * (gram(g) + gram(u)) + gram(dy) * gram(h))
    own_ref[...] = jnp.full(own_ref.shape, own, F32)


def group_kernel(
    place_ref, scale_ref, x_ref, dy_ref, g_ref, u_ref, h_ref, *refs
):
    got_refs, swap_refs = refs[: NY - 1], refs[NY - 1 : 2 * NY - 2]
    wg_ref, wu_ref, wd_ref, out_ref, xs, dys, x_part, dy_part = refs[2 * NY - 2 :]
    tokens, width = x_ref.shape
    others = NY - 1
    part = width // NY
    first = place_ref[0] == 0
    for e in range(others):
        rows = slice(e * tokens, (e + 1) * tokens)
        a, b = got_refs[e][...], swap_refs[e][...]
        xs[rows, :] = jnp.where(first, a, b).astype(BF16)
        dys[rows, :] = jnp.where(first, b, a).astype(BF16)
    for k in range(NY):
        @pl.when(place_ref[1] == k)
        def _():
            cols = slice(k * part, (k + 1) * part)
            x_part[:tokens, :] = x_ref[:, cols]
            dy_part[:tokens, :] = dy_ref[:, cols]
            x_part[tokens:, :] = xs[:, cols]
            dy_part[tokens:, :] = dys[:, cols]
    g, u, h = forward(xs[...], dys[...], wg_ref[...], wu_ref[...], wd_ref[...])
    rows = part // NZ
    for m, (left, mine, other) in enumerate(
        ((x_part, g_ref, g), (x_part, u_ref, u), (dy_part, h_ref, h))
    ):
        scaled = [(mine[...].astype(F32) * scale_ref[0, 0:1, 0:1]).astype(BF16)]
        for e in range(others):
            piece = other[e * tokens : (e + 1) * tokens].astype(F32)
            scaled.append((piece * scale_ref[e + 1, 0:1, 0:1]).astype(BF16))
        grad = dot(left[...], jnp.concatenate(scaled, axis=0), ((0,), (0,)))
        for z in range(NZ):
            out_ref[z, m * rows : (m + 1) * rows, :] = grad[z * rows : (z + 1) * rows]


def forward(x, dy, gate_weight, up_weight, down_weight):
    gate_pre = dot(x, gate_weight, ((1,), (0,)))
    up_pre = dot(x, up_weight, ((1,), (0,)))
    activated, gelu_slope = gelu_parts(gate_pre)
    hidden = (activated * up_pre).astype(BF16)
    hidden_grad = dot(dy, down_weight, ((1,), (0,)))
    gate_back = (hidden_grad * up_pre * gelu_slope).astype(BF16)
    up_back = (hidden_grad * activated).astype(BF16)
    return gate_back, up_back, hidden


def gram(matrix):
    return dot(matrix, matrix, ((1,), (1,)))


def per_device(inputs, gate_weight, up_weight, down_weight, out_grad, later_norms):
    y = lax.axis_index("y")
    x = lax.axis_index("x")
    core = lax.axis_index("core")
    tokens, width = inputs.shape
    ff = gate_weight.shape[1]
    weights = (gate_weight, up_weight, down_weight)
    vmem = pl.BlockSpec(memory_space=pltpu.VMEM)
    params = pltpu.CompilerParams(vmem_limit_bytes=VMEM_LIMIT)

    mine = jnp.where(core == 0, inputs, out_grad).astype(F32)
    got = [shift(mine, "y", k) for k in (1, 3, 2)]

    hidden_type = jax.ShapeDtypeStruct((tokens, ff), BF16)
    gate_back, up_back, hidden, own = pl.pallas_call(
        own_kernel,
        out_shape=[hidden_type, hidden_type, hidden_type, jax.ShapeDtypeStruct((8, 128), F32)],
        in_specs=[vmem] * 5,
        out_specs=[vmem] * 4,
        compiler_params=params,
        name="own_example",
    )(inputs, out_grad, *weights)
    own = own + shift(own, "core", 1)
    own = own + (shift(own, "x", 1) + shift(own, "x", 3)) + shift(own, "x", 2)
    clip = jnp.minimum(1.0, CLIP_NORM / jnp.sqrt(later_norms[:, None] + own))
    scale = clip * math.sqrt(width * ff * NX * NC / (NY * NZ))
    scales = jnp.stack([scale] + [shift(scale, "y", k) for k in (1, 3, 2)])

    swapped = [shift(a, "core", 1) for a in got]
    part = width // NY
    grads = pl.pallas_call(
        group_kernel,
        out_shape=jax.ShapeDtypeStruct((NZ, 3 * part // NZ, ff), F32),
        in_specs=[pl.BlockSpec(memory_space=pltpu.SMEM)] + [vmem] * (6 + 2 * (NY - 1) + 3),
        out_specs=vmem,
        scratch_shapes=[
            pltpu.VMEM(((NY - 1) * tokens, width), BF16),
            pltpu.VMEM(((NY - 1) * tokens, width), BF16),
            pltpu.VMEM((NY * tokens, part), BF16),
            pltpu.VMEM((NY * tokens, part), BF16),
        ],
        compiler_params=params,
        name="group_gradients",
    )(
        jnp.stack([core, y]).astype(jnp.int32), scales, inputs, out_grad, gate_back, up_back, hidden,
        *got, *swapped, *weights,
    )
    grads = lax.psum_scatter(grads, "z", scatter_dimension=0, tiled=False)
    rows = part // NZ

    partial = dot(gate_back, gate_weight, ((1,), (1,))) + dot(up_back, up_weight, ((1,), (1,)))
    partial = partial.reshape(NX, NC, tokens // (NX * NC), width)
    keep = lax.dynamic_index_in_dim(partial, core, 1, False)
    give = lax.dynamic_index_in_dim(partial, 1 - core, 1, False)
    keep = keep + shift(give, "core", 1)
    total = lax.dynamic_index_in_dim(keep, x, 0, False)
    for k in (1, 3, 2):
        total = total + shift(lax.dynamic_index_in_dim(keep, (x + k) % NX, 0, False), "x", k)
    return (total.astype(BF16), grads[:rows], grads[rows : 2 * rows], grads[2 * rows :])


def solution(mesh):
    fine = Mesh(mesh.devices.reshape(NY, NZ, NX, NC), ("y", "z", "x", "core"))
    dp, tensor = ("y", "z"), ("x", "core")
    in_specs = (
        P(dp, None),
        P(None, tensor),
        P(None, tensor),
        P(None, tensor),
        P(dp, None),
        P(dp),
    )
    out_specs = (P(dp + tensor, None), P(dp, tensor), P(dp, tensor), P(dp, tensor))
    return jax.shard_map(
        per_device, mesh=fine, in_specs=in_specs, out_specs=out_specs, check_vma=False
    )
```

time: 315 us -> 143 us (0.45)
  waiting for transfers between devices: 255 us -> 73.7 us
  starting transfers between devices: 0.08 us -> 18.5 us
  blocking collectives: 15.2 us -> 0 us
  matrix products: 15.6 us -> 0.99 us
  Pallas kernels: 0 us -> 13.8 us
  local copies, waits for them, and re-layouts: 7.86 us -> 17.5 us
    unnamed x3 -> x1, waiting for transfers between devices: 248 us -> 0.02 us
    ppermute x0 -> x17, waiting for transfers between devices: none -> 43.3 us  [shift(): lax.ppermute(array, axis, [(i, (i + step) % size) for i in range(size)])]
    reduce_scatter x1, waiting for transfers between devices: 7.37 us -> 30.4 us  [per_device(): grads = lax.psum_scatter(grads, 'z', scatter_dimension=0, tiled=False)]
    ppermute x0 -> x17, starting transfers between devices: none -> 18.4 us  [shift(): lax.ppermute(array, axis, [(i, (i + step) % size) for i in range(size)])]
    psum x1 -> x0, blocking collectives: 15.2 us -> none  [per_device(): own_norm = lax.psum(own_part, 'tensor')]
    dot_general x13 -> x2, matrix products: 15.6 us -> 0.99 us  [dot(): lax.dot_general(left, right, (dims, ((), ())), preferred_element_type=F32)]
    pallas_call x0 -> x2, Pallas kernels: none -> 13.8 us  [the longest x1 10.4 us: per_device(): pl.pallas_call(group_kernel, out_shape=jax.ShapeDtypeStruct((NZ, 3 * part...]
    unnamed x18 -> x15, local copies, waits for them, and re-layouts: 7.86 us -> 15.6 us
  transfers between devices with their start and end apart: 2 -> 18, of which waited for: 2 -> 13; matrix products, arithmetic and copies ran while one was open for 4% -> 9% of each run, Pallas kernels for 0% -> 2%
where the time goes in v1:
time: 143 us; the launch traced here: 141 us
  waiting for transfers between devices  73.7 us (52%)
  starting transfers between devices  18.5 us (13%)
  local copies, waits for them, and re-layouts  17.5 us (12%)
  between operations  14.8 us (10%)
  Pallas kernels  13.8 us (10%)
  other arithmetic  1.77 us (1%)
    ppermute x17, waiting for transfers between devices, shift(): lax.ppermute(array, axis, [(i, (i + step) % size) for i in range(size)])  43.3 us
    reduce_scatter x1, waiting for transfers between devices, per_device(): grads = lax.psum_scatter(grads, 'z', scatter_dimension=0, tiled=False)  30.4 us
    ppermute x17, starting transfers between devices, shift(): lax.ppermute(array, axis, [(i, (i + step) % size) for i in range(size)])  18.4 us
    unnamed x15, local copies, waits for them, and re-layouts  15.6 us
    pallas_call x1, Pallas kernels, per_device(): pl.pallas_call(group_kernel, out_shape=jax.ShapeDtypeStruct((NZ, 3 * part...  10.4 us
    pallas_call x1, Pallas kernels, per_device(): pl.pallas_call(own_kernel, out_shape=[hidden_type, hidden_type, hidden_ty...  3.4 us
  transfers between devices with their start and end apart: 18, of which 13 were waited for; matrix products, arithmetic and copies ran while one was open for 9% of the time, Pallas kernels for 2%

profile of v1, /device:TPU:96, one launch (start us, length us, event | category | flops | bytes accessed | tf_op | source)
XLA Modules:
  0.0 141.0 jit_solution(10119751196168599856)
XLA Ops:
  7.2 0.0 reduce-scatter.2.cloned.1.call-start
  7.2 1.0 select_convert_fusion
  8.2 1.7 %collective-permute-start.11 = (f32[128,1152]{1,0:T(8,128)S(1)}, f32[128,1152]{1,0:T(8,128)}, u32[]{:S(2)}, u32[]{:S(2)}) collective-permute-start(f32[128,1152]{1,0:T(8,128)S(1)} %select_convert_fusion), channel_id=1, source_target_pairs={{0,64},{64,128},{128,192},{192,0},{1,65},{65,129},{129,193},{193,1... | collective-permute-start | bytes 1769480 | tf_op jit(solution)/shard_map/ppermute | solution.py:29
  9.9 1.7 %collective-permute-start.12 = (f32[128,1152]{1,0:T(8,128)S(1)}, f32[128,1152]{1,0:T(8,128)}, u32[]{:S(2)}, u32[]{:S(2)}) collective-permute-start(f32[128,1152]{1,0:T(8,128)S(1)} %select_convert_fusion), channel_id=1, source_target_pairs={{0,192},{64,0},{128,64},{192,128},{1,193},{65,1},{129,65},{193,129... | collective-permute-start | bytes 1769480 | tf_op jit(solution)/shard_map/ppermute | solution.py:29
  11.5 2.0 %collective-permute-start.13 = (f32[128,1152]{1,0:T(8,128)S(1)}, f32[128,1152]{1,0:T(8,128)}, u32[]{:S(2)}, u32[]{:S(2)}) collective-permute-start(f32[128,1152]{1,0:T(8,128)S(1)} %select_convert_fusion), channel_id=1, source_target_pairs={{0,128},{64,192},{128,0},{192,64},{1,129},{65,193},{129,1},{193,65... | collective-permute-start | bytes 1769480 | tf_op jit(solution)/shard_map/ppermute | solution.py:29
  13.5 11.2 %collective-permute-done.11.refs_0_ = f32[128,1152]{1,0:T(8,128)} collective-permute-done((f32[128,1152]{1,0:T(8,128)S(1)}, f32[128,1152]{1,0:T(8,128)}, u32[]{:S(2)}, u32[]{:S(2)}) %collective-permute-start.11) | collective-permute-done | bytes 589856 | tf_op jit(solution)/shard_map/ppermute | solution.py:29
  24.8 0.0 collective-permute-start.14
  24.8 11.9 %collective-permute-done.12.refs_1_ = f32[128,1152]{1,0:T(8,128)} collective-permute-done((f32[128,1152]{1,0:T(8,128)S(1)}, f32[128,1152]{1,0:T(8,128)}, u32[]{:S(2)}, u32[]{:S(2)}) %collective-permute-start.12) | collective-permute-done | bytes 589856 | tf_op jit(solution)/shard_map/ppermute | solution.py:29
  36.7 0.0 collective-permute-start.15
  36.7 1.9 %collective-permute-done.13.refs_2_ = f32[128,1152]{1,0:T(8,128)} collective-permute-done((f32[128,1152]{1,0:T(8,128)S(1)}, f32[128,1152]{1,0:T(8,128)}, u32[]{:S(2)}, u32[]{:S(2)}) %collective-permute-start.13) | collective-permute-done | bytes 589856 | tf_op jit(solution)/shard_map/ppermute | solution.py:29
  38.6 0.0 collective-permute-start.16
  38.6 2.9 %copy.10.wg_ref.refs_6_ = bf16[1152,864]{1,0:T(8,128)(2,1)S(1)} copy(bf16[1152,864]{0,1:T(8,128)(2,1)} %param.7) | data formatting | bytes 3981312 | tf_op args[1]
  41.5 0.0 copy-start
  41.5 4.4 %copy.11.wu_ref.refs_7_ = bf16[1152,864]{1,0:T(8,128)(2,1)} copy(bf16[1152,864]{0,1:T(8,128)(2,1)} %param.8) | data formatting | bytes 3981312 | tf_op args[2]
  45.9 0.0 copy-start.2
  45.9 0.0 copy-start.3
  45.9 4.1 %copy.12.wd_ref.refs_8_ = bf16[1152,864]{1,0:T(8,128)(2,1)} copy(bf16[1152,864]{0,1:T(8,128)(2,1)} %param.9) | data formatting | bytes 3981312 | tf_op args[3]
  50.0 0.0 copy-done
  50.0 0.0 copy-done.2
  50.0 0.0 copy-done.3
  50.0 0.0 copy-start.1
  50.1 1.6 %copy-done.1 = bf16[1152,864]{1,0:T(8,128)(2,1)S(1)} copy-done((bf16[1152,864]{1,0:T(8,128)(2,1)S(1)}, bf16[1152,864]{1,0:T(8,128)(2,1)}, u32[]{:S(2)}) %copy-start.1) | copy-done | bytes 1990680
  51.6 3.4 %own_example.1 = (bf16[128,864]{1,0:T(8,128)(2,1)S(1)}, bf16[128,864]{1,0:T(8,128)(2,1)S(1)}, bf16[128,864]{1,0:T(8,128)(2,1)S(1)}, f32[8,128]{1,0:T(8,128)S(1)}) custom-call(bf16[128,1152]{1,0:T(8,128)(2,1)S(1)} %copy-done.2, bf16[128,1152]{1,0:T(8,128)(2,1)S(1)} %copy-done.3, bf16[1152,864]{1,0:T(8,128)(2,1)S(1)} %copy.10.wg_ref.refs_6_, ...), custom_call_target="tpu_custom_call" | custom-call | tf_op jit(solution)/shard_map/own_example/pallas_call | solution.py:112
  55.0 0.6 collective-permute-start.4
  55.6 0.8 collective-permute-done.4
  56.5 1.5 %collective-permute-start.5 = (f32[8,128]{1,0:T(8,128)S(1)}, f32[8,128]{1,0:T(8,128)S(1)}, u32[]{:S(2)}, u32[]{:S(2)}) collective-permute-start(f32[8,128]{1,0:T(8,128)S(1)} %add.98), channel_id=1, source_target_pairs={{0,2},{2,4},{4,6},{6,0},{1,3},{3,5},{5,7},{7,1},{8,10},{10,12},{12... | collective-permute-start | bytes 12296 | tf_op jit(solution)/shard_map/ppermute | solution.py:29
  58.0 1.7 %collective-permute-start.6 = (f32[8,128]{1,0:T(8,128)S(1)}, f32[8,128]{1,0:T(8,128)S(1)}, u32[]{:S(2)}, u32[]{:S(2)}) collective-permute-start(f32[8,128]{1,0:T(8,128)S(1)} %add.98), channel_id=1, source_target_pairs={{0,6},{2,0},{4,2},{6,4},{1,7},{3,1},{5,3},{7,5},{8,14},{10,8},{12,... | collective-permute-start | bytes 12296 | tf_op jit(solution)/shard_map/ppermute | solution.py:29
  59.7 1.6 %collective-permute-done.5 = f32[8,128]{1,0:T(8,128)S(1)} collective-permute-done((f32[8,128]{1,0:T(8,128)S(1)}, f32[8,128]{1,0:T(8,128)S(1)}, u32[]{:S(2)}, u32[]{:S(2)}) %collective-permute-start.5) | collective-permute-done | bytes 4128 | tf_op jit(solution)/shard_map/ppermute | solution.py:29
  61.3 1.8 %collective-permute-start.7 = (f32[8,128]{1,0:T(8,128)S(1)}, f32[8,128]{1,0:T(8,128)S(1)}, u32[]{:S(2)}, u32[]{:S(2)}) collective-permute-start(f32[8,128]{1,0:T(8,128)S(1)} %add.98), channel_id=1, source_target_pairs={{0,4},{2,6},{4,0},{6,2},{1,5},{3,7},{5,1},{7,3},{8,12},{10,14},{12... | collective-permute-start | bytes 12296 | tf_op jit(solution)/shard_map/ppermute | solution.py:29
  63.7 0.0 collective-permute-done.6
  63.8 2.6 %collective-permute-done.7 = f32[8,128]{1,0:T(8,128)S(1)} collective-permute-done((f32[8,128]{1,0:T(8,128)S(1)}, f32[8,128]{1,0:T(8,128)S(1)}, u32[]{:S(2)}, u32[]{:S(2)}) %collective-permute-start.7) | collective-permute-done | bytes 4128 | tf_op jit(solution)/shard_map/ppermute | solution.py:29
  66.4 1.2 collective-permute-start.8
  67.6 2.1 %collective-permute-start.9 = (f32[8,128]{1,0:T(8,128)S(1)}, f32[8,128]{1,0:T(8,128)S(1)}, u32[]{:S(2)}, u32[]{:S(2)}) collective-permute-start(f32[8,128]{1,0:T(8,128)S(1)} %minimum_multiply_fusion), channel_id=1, source_target_pairs={{0,192},{64,0},{128,64},{192,128},{1,193},{65,1},{129,65},{193,129... | collective-permute-start | bytes 12296 | tf_op jit(solution)/shard_map/ppermute | solution.py:29
  69.7 1.6 %collective-permute-done.8 = f32[8,128]{1,0:T(8,128)S(1)} collective-permute-done((f32[8,128]{1,0:T(8,128)S(1)}, f32[8,128]{1,0:T(8,128)S(1)}, u32[]{:S(2)}, u32[]{:S(2)}) %collective-permute-start.8) | collective-permute-done | bytes 4128 | tf_op jit(solution)/shard_map/ppermute | solution.py:29
  71.3 0.2 collective-permute-start.10
  71.5 0.1 pad_add_fusion.place_ref
  71.6 0.0 collective-permute-done.9
  71.6 4.9 %collective-permute-done.10 = f32[8,128]{1,0:T(8,128)S(1)} collective-permute-done((f32[8,128]{1,0:T(8,128)S(1)}, f32[8,128]{1,0:T(8,128)S(1)}, u32[]{:S(2)}, u32[]{:S(2)}) %collective-permute-start.10) | collective-permute-done | bytes 4128 | tf_op jit(solution)/shard_map/ppermute | solution.py:29
  76.4 0.0 collective-permute-done.14.refs_3_
  76.4 0.0 collective-permute-done.15.refs_4_
  76.4 0.0 collective-permute-done.16.refs_5_
  76.4 10.4 %group_gradients.1 = f32[8,108,864]{2,1,0:T(8,128)} custom-call(s32[2]{0:T(128)S(1)} %pad_add_fusion.place_ref, f32[4,8,128]{2,1,0:T(8,128)S(1)} %pad_maximum_fusion.scale_ref, bf16[128,1152]{1,0:T(8,128)(2,1)S(1)} %copy-done.2, bf16[128,1152]{1,0:T(8,128)(2,1)S(1)} %copy-done.3, bf16[128,864]{1,0:T(8,128)(2,1)S(1)} %get-tuple-element.8.g_ref, ...), custom_call_target="tpu_custom_call" | custom-call | tf_op jit(solution)/shard_map/group_gradients/pallas_call | solution.py:128
  86.8 0.0 copy-start.4
  86.8 0.0 reduce-scatter.2.cloned.1.call-update
  86.8 1.5 %copy-done.4 = bf16[1152,864]{0,1:T(8,128)(2,1)S(1)} copy-done((bf16[1152,864]{0,1:T(8,128)(2,1)S(1)}, bf16[1152,864]{0,1:T(8,128)(2,1)}, u32[]{:S(2)}) %copy-start.4) | copy-done | bytes 1990680
  88.4 0.0 copy-start.5
  88.4 0.5 fusion.3
  88.9 1.1 copy-done.5
  89.9 0.5 convolution_add_fusion
  90.5 0.1 collective-permute-start
  90.6 1.5 %collective-permute-done = f32[4,16,1152]{2,1,0:T(8,128)S(1)} collective-permute-done((f32[4,16,1152]{2,1,0:T(8,128)S(1)}, f32[4,16,1152]{2,1,0:T(8,128)S(1)}, u32[]{:S(2)}, u32[]{:S(2)}) %collective-permute-start) | collective-permute-done | bytes 294944 | tf_op jit(solution)/shard_map/ppermute | solution.py:29
  92.2 0.4 collective-permute-start.1
  92.6 3.0 %collective-permute-start.2 = (f32[16,1152]{1,0:T(8,128)S(1)}, f32[16,1152]{1,0:T(8,128)S(1)}, u32[]{:S(2)}, u32[]{:S(2)}) collective-permute-start(f32[16,1152]{1,0:T(8,128)S(1)} %get-tuple-element.17), channel_id=1, source_target_pairs={{0,6},{2,0},{4,2},{6,4},{1,7},{3,1},{5,3},{7,5},{8,14},{10,8},{12,... | collective-permute-start | bytes 221192 | tf_op jit(solution)/shard_map/ppermute | solution.py:29
  95.5 0.6 collective-permute-start.3
  96.1 1.7 %collective-permute-done.1 = f32[16,1152]{1,0:T(8,128)S(1)} collective-permute-done((f32[16,1152]{1,0:T(8,128)S(1)}, f32[16,1152]{1,0:T(8,128)S(1)}, u32[]{:S(2)}, u32[]{:S(2)}) %collective-permute-start.1) | collective-permute-done | bytes 73760 | tf_op jit(solution)/shard_map/ppermute | solution.py:29
  97.9 0.8 collective-permute-done.2
  98.7 2.7 %collective-permute-done.3 = f32[16,1152]{1,0:T(8,128)S(1)} collective-permute-done((f32[16,1152]{1,0:T(8,128)S(1)}, f32[16,1152]{1,0:T(8,128)S(1)}, u32[]{:S(2)}, u32[]{:S(2)}) %collective-permute-start.3) | collective-permute-done | bytes 73760 | tf_op jit(solution)/shard_map/ppermute | solution.py:29
  101.4 0.6 fusion.2
  102.0 30.4 %reduce-scatter.2.cloned.1.call-done = f32[1,108,864]{2,1,0:T(8,128)} async-done(((f32[8,108,864]{2,1,0:T(8,128)}), f32[1,108,864]{2,1,0:T(8,128)}) %reduce-scatter.2.cloned.1.call-update) | async-done | bytes 373264 | tf_op jit(solution)/shard_map/reduce_scatter | solution.py:145
  132.4 1.8 %slice_bitcast_fusion = (f32[36,864]{1,0:T(8,128)}, f32[36,864]{1,0:T(8,128)}, f32[36,864]{1,0:T(8,128)}) fusion(f32[1,108,864]{2,1,0:T(8,128)} %reduce-scatter.2.cloned.1.call-done), kind=kLoop, calls=%fused_computation.4 | loop fusion | bytes 746496 | tf_op jit(solution)/shard_map/slice | solution.py:156
  (6 shorter events, 0.1 us)
Async XLA Ops:
  7.2 125.2 %reduce-scatter.2.cloned.1.call-start = ((), (), s32[]{:S(2)}) async-start(), calls=%async_computation.1 | async-start | bytes 3612672 | tf_op jit(solution)/shard_map/reduce_scatter | solution.py:145
  8.2 16.5 %collective-permute-start.11 = (f32[128,1152]{1,0:T(8,128)S(1)}, f32[128,1152]{1,0:T(8,128)}, u32[]{:S(2)}, u32[]{:S(2)}) collective-permute-start(f32[128,1152]{1,0:T(8,128)S(1)} %select_convert_fusion), channel_id=1, source_target_pairs={{0,64},{64,128},{128,192},{192,0},{1,65},{65,129},{129,193},{193,1... | collective-permute-start | bytes 1769480 | tf_op jit(solution)/shard_map/ppermute | solution.py:29
  9.9 26.8 %collective-permute-start.12 = (f32[128,1152]{1,0:T(8,128)S(1)}, f32[128,1152]{1,0:T(8,128)}, u32[]{:S(2)}, u32[]{:S(2)}) collective-permute-start(f32[128,1152]{1,0:T(8,128)S(1)} %select_convert_fusion), channel_id=1, source_target_pairs={{0,192},{64,0},{128,64},{192,128},{1,193},{65,1},{129,65},{193,129... | collective-permute-start | bytes 1769480 | tf_op jit(solution)/shard_map/ppermute | solution.py:29
  11.5 27.0 %collective-permute-start.13 = (f32[128,1152]{1,0:T(8,128)S(1)}, f32[128,1152]{1,0:T(8,128)}, u32[]{:S(2)}, u32[]{:S(2)}) collective-permute-start(f32[128,1152]{1,0:T(8,128)S(1)} %select_convert_fusion), channel_id=1, source_target_pairs={{0,128},{64,192},{128,0},{192,64},{1,129},{65,193},{129,1},{193,65... | collective-permute-start | bytes 1769480 | tf_op jit(solution)/shard_map/ppermute | solution.py:29
  24.8 51.7 %collective-permute-start.14 = (f32[128,1152]{1,0:T(8,128)}, f32[128,1152]{1,0:T(8,128)}, u32[]{:S(2)}, u32[]{:S(2)}) collective-permute-start(f32[128,1152]{1,0:T(8,128)} %collective-permute-done.11.refs_0_), channel_id=1, source_target_pairs={{0,1},{1,0},{2,3},{3,2},{4,5},{5,4},{6,7},{7,6},{8,9},{9,8},{10,11... | collective-permute-start | bytes 1769480 | tf_op jit(solution)/shard_map/ppermute | solution.py:29
  36.7 39.7 %collective-permute-start.15 = (f32[128,1152]{1,0:T(8,128)}, f32[128,1152]{1,0:T(8,128)}, u32[]{:S(2)}, u32[]{:S(2)}) collective-permute-start(f32[128,1152]{1,0:T(8,128)} %collective-permute-done.12.refs_1_), channel_id=1, source_target_pairs={{0,1},{1,0},{2,3},{3,2},{4,5},{5,4},{6,7},{7,6},{8,9},{9,8},{10,11... | collective-permute-start | bytes 1769480 | tf_op jit(solution)/shard_map/ppermute | solution.py:29
  38.6 37.8 %collective-permute-start.16 = (f32[128,1152]{1,0:T(8,128)}, f32[128,1152]{1,0:T(8,128)}, u32[]{:S(2)}, u32[]{:S(2)}) collective-permute-start(f32[128,1152]{1,0:T(8,128)} %collective-permute-done.13.refs_2_), channel_id=1, source_target_pairs={{0,1},{1,0},{2,3},{3,2},{4,5},{5,4},{6,7},{7,6},{8,9},{9,8},{10,11... | collective-permute-start | bytes 1769480 | tf_op jit(solution)/shard_map/ppermute | solution.py:29
  41.5 8.6 %copy-start = (bf16[1152,864]{1,0:T(8,128)(2,1)}, bf16[1152,864]{1,0:T(8,128)(2,1)S(1)}, u32[]{:S(2)}) copy-start(bf16[1152,864]{1,0:T(8,128)(2,1)S(1)} %copy.10.wg_ref.refs_6_) | copy-start | bytes 5971972
  45.9 4.1 %copy-start.2 = (bf16[128,1152]{1,0:T(8,128)(2,1)S(1)}, bf16[128,1152]{1,0:T(8,128)(2,1)}, u32[]{:S(2)}) copy-start(bf16[128,1152]{1,0:T(8,128)(2,1)} %x_ref.3) | copy-start | bytes 884740
  45.9 4.1 %copy-start.3 = (bf16[128,1152]{1,0:T(8,128)(2,1)S(1)}, bf16[128,1152]{1,0:T(8,128)(2,1)}, u32[]{:S(2)}) copy-start(bf16[128,1152]{1,0:T(8,128)(2,1)} %dy_ref.3) | copy-start | bytes 884740
  50.0 1.6 %copy-start.1 = (bf16[1152,864]{1,0:T(8,128)(2,1)S(1)}, bf16[1152,864]{1,0:T(8,128)(2,1)}, u32[]{:S(2)}) copy-start(bf16[1152,864]{1,0:T(8,128)(2,1)} %copy.11.wu_ref.refs_7_) | copy-start | bytes 5971972
  55.0 1.4 %collective-permute-start.4 = (f32[8,128]{1,0:T(8,128)S(1)}, f32[8,128]{1,0:T(8,128)S(1)}, u32[]{:S(2)}, u32[]{:S(2)}) collective-permute-start(f32[8,128]{1,0:T(8,128)S(1)} %get-tuple-element.10), channel_id=1, source_target_pairs={{0,1},{1,0},{2,3},{3,2},{4,5},{5,4},{6,7},{7,6},{8,9},{9,8},{10,11... | collective-permute-start | bytes 12296 | tf_op jit(solution)/shard_map/ppermute | solution.py:29
  56.5 4.8 %collective-permute-start.5 = (f32[8,128]{1,0:T(8,128)S(1)}, f32[8,128]{1,0:T(8,128)S(1)}, u32[]{:S(2)}, u32[]{:S(2)}) collective-permute-start(f32[8,128]{1,0:T(8,128)S(1)} %add.98), channel_id=1, source_target_pairs={{0,2},{2,4},{4,6},{6,0},{1,3},{3,5},{5,7},{7,1},{8,10},{10,12},{12... | collective-permute-start | bytes 12296 | tf_op jit(solution)/shard_map/ppermute | solution.py:29
  58.0 5.8 %collective-permute-start.6 = (f32[8,128]{1,0:T(8,128)S(1)}, f32[8,128]{1,0:T(8,128)S(1)}, u32[]{:S(2)}, u32[]{:S(2)}) collective-permute-start(f32[8,128]{1,0:T(8,128)S(1)} %add.98), channel_id=1, source_target_pairs={{0,6},{2,0},{4,2},{6,4},{1,7},{3,1},{5,3},{7,5},{8,14},{10,8},{12,... | collective-permute-start | bytes 12296 | tf_op jit(solution)/shard_map/ppermute | solution.py:29
  61.3 5.1 %collective-permute-start.7 = (f32[8,128]{1,0:T(8,128)S(1)}, f32[8,128]{1,0:T(8,128)S(1)}, u32[]{:S(2)}, u32[]{:S(2)}) collective-permute-start(f32[8,128]{1,0:T(8,128)S(1)} %add.98), channel_id=1, source_target_pairs={{0,4},{2,6},{4,0},{6,2},{1,5},{3,7},{5,1},{7,3},{8,12},{10,14},{12... | collective-permute-start | bytes 12296 | tf_op jit(solution)/shard_map/ppermute | solution.py:29
  66.4 4.9 %collective-permute-start.8 = (f32[8,128]{1,0:T(8,128)S(1)}, f32[8,128]{1,0:T(8,128)S(1)}, u32[]{:S(2)}, u32[]{:S(2)}) collective-permute-start(f32[8,128]{1,0:T(8,128)S(1)} %minimum_multiply_fusion), channel_id=1, source_target_pairs={{0,64},{64,128},{128,192},{192,0},{1,65},{65,129},{129,193},{193,1... | collective-permute-start | bytes 12296 | tf_op jit(solution)/shard_map/ppermute | solution.py:29
  67.6 3.9 %collective-permute-start.9 = (f32[8,128]{1,0:T(8,128)S(1)}, f32[8,128]{1,0:T(8,128)S(1)}, u32[]{:S(2)}, u32[]{:S(2)}) collective-permute-start(f32[8,128]{1,0:T(8,128)S(1)} %minimum_multiply_fusion), channel_id=1, source_target_pairs={{0,192},{64,0},{128,64},{192,128},{1,193},{65,1},{129,65},{193,129... | collective-permute-start | bytes 12296 | tf_op jit(solution)/shard_map/ppermute | solution.py:29
  71.3 5.1 %collective-permute-start.10 = (f32[8,128]{1,0:T(8,128)S(1)}, f32[8,128]{1,0:T(8,128)S(1)}, u32[]{:S(2)}, u32[]{:S(2)}) collective-permute-start(f32[8,128]{1,0:T(8,128)S(1)} %minimum_multiply_fusion), channel_id=1, source_target_pairs={{0,128},{64,192},{128,0},{192,64},{1,129},{65,193},{129,1},{193,65... | collective-permute-start | bytes 12296 | tf_op jit(solution)/shard_map/ppermute | solution.py:29
  86.8 1.6 %copy-start.4 = (bf16[1152,864]{0,1:T(8,128)(2,1)S(1)}, bf16[1152,864]{0,1:T(8,128)(2,1)}, u32[]{:S(2)}) copy-start(bf16[1152,864]{0,1:T(8,128)(2,1)} %param.7) | copy-start | bytes 5971972
  88.4 1.6 %copy-start.5 = (bf16[1152,864]{0,1:T(8,128)(2,1)S(1)}, bf16[1152,864]{0,1:T(8,128)(2,1)}, u32[]{:S(2)}) copy-start(bf16[1152,864]{0,1:T(8,128)(2,1)} %param.8) | copy-start | bytes 5971972
  90.5 1.7 %collective-permute-start = (f32[4,16,1152]{2,1,0:T(8,128)S(1)}, f32[4,16,1152]{2,1,0:T(8,128)S(1)}, u32[]{:S(2)}, u32[]{:S(2)}) collective-permute-start(f32[4,16,1152]{2,1,0:T(8,128)S(1)} %dynamic-slice_bitcast_fusion), channel_id=1, source_target_pairs={{0,1},{1,0},{2,3},{3,2},{4,5},{5,4},{6,7},{7,6},{8,9},{9,8},{10,11... | collective-permute-start | bytes 884744 | tf_op jit(solution)/shard_map/ppermute | solution.py:29
  92.2 5.6 %collective-permute-start.1 = (f32[16,1152]{1,0:T(8,128)S(1)}, f32[16,1152]{1,0:T(8,128)S(1)}, u32[]{:S(2)}, u32[]{:S(2)}) collective-permute-start(f32[16,1152]{1,0:T(8,128)S(1)} %get-tuple-element.15), channel_id=1, source_target_pairs={{0,2},{2,4},{4,6},{6,0},{1,3},{3,5},{5,7},{7,1},{8,10},{10,12},{12... | collective-permute-start | bytes 221192 | tf_op jit(solution)/shard_map/ppermute | solution.py:29
  92.6 6.1 %collective-permute-start.2 = (f32[16,1152]{1,0:T(8,128)S(1)}, f32[16,1152]{1,0:T(8,128)S(1)}, u32[]{:S(2)}, u32[]{:S(2)}) collective-permute-start(f32[16,1152]{1,0:T(8,128)S(1)} %get-tuple-element.17), channel_id=1, source_target_pairs={{0,6},{2,0},{4,2},{6,4},{1,7},{3,1},{5,3},{7,5},{8,14},{10,8},{12,... | collective-permute-start | bytes 221192 | tf_op jit(solution)/shard_map/ppermute | solution.py:29
  95.5 5.9 %collective-permute-start.3 = (f32[16,1152]{1,0:T(8,128)S(1)}, f32[16,1152]{1,0:T(8,128)S(1)}, u32[]{:S(2)}, u32[]{:S(2)}) collective-permute-start(f32[16,1152]{1,0:T(8,128)S(1)} %get-tuple-element.16), channel_id=1, source_target_pairs={{0,4},{2,6},{4,0},{6,2},{1,5},{3,7},{5,1},{7,3},{8,12},{10,14},{12... | collective-permute-start | bytes 221192 | tf_op jit(solution)/shard_map/ppermute | solution.py:29
Sparse Core Ops, SparseCore 0:
  87.0 45.3 reduce-scatter.1

commit v2 on v0

v2 whole, which is shorter than its diff:
```python
import functools
import math

import jax
import jax.numpy as jnp
from jax import lax
from jax.experimental import pallas as pl
from jax.experimental.pallas import tpu as pltpu
from jax.sharding import Mesh, PartitionSpec as P

CLIP_NORM = 1.8
GELU_C = 0.7978845608028654
NY, NZ, NX, NC = 4, 8, 4, 2
OWN_MIB = 48
F32 = jnp.float32
BF16 = jnp.bfloat16


def gelu_parts(pre):
    tangent = jnp.tanh(GELU_C * (pre + 0.044715 * pre * pre * pre))
    activated = 0.5 * pre * (1.0 + tangent)
    gelu_slope = 0.5 * (1.0 + tangent) + 0.5 * pre * (1.0 - tangent * tangent) * GELU_C * (
        1.0 + 3.0 * 0.044715 * pre * pre
    )
    return (activated, gelu_slope)


def shift(array, axis, step):
    size = lax.axis_size(axis)
    return lax.ppermute(array, axis, [(i, (i + step) % size) for i in range(size)])


def dot(left, right, dims):
    return lax.dot_general(left, right, (dims, ((), ())), preferred_element_type=F32)


def forward(x, dy, gate_weight, up_weight, down_weight):
    gate_pre = dot(x, gate_weight, ((1,), (1,)))
    up_pre = dot(x, up_weight, ((1,), (1,)))
    activated, gelu_slope = gelu_parts(gate_pre)
    hidden = (activated * up_pre).astype(BF16)
    hidden_grad = dot(dy, down_weight, ((1,), (1,)))
    gate_back = (hidden_grad * up_pre * gelu_slope).astype(BF16)
    up_back = (hidden_grad * activated).astype(BF16)
    return gate_back, up_back, hidden


def gram(matrix):
    return dot(matrix, matrix, ((1,), (1,)))


def prepare_kernel(x_ref, dy_ref, out_ref, token_ref):
    token_ref[...] = jnp.zeros(token_ref.shape, F32)
    first = lax.axis_index("core") == 0

    @pl.when(first)
    def _():
        out_ref[...] = x_ref[...].astype(F32)

    @pl.when(jnp.logical_not(first))
    def _():
        out_ref[...] = dy_ref[...].astype(F32)


def own_kernel(
    x_hbm, dy_hbm, wg_hbm, wu_hbm, wd_hbm, token_ref, g_ref, u_ref, h_ref, keep_ref, give_ref, wg, wu, wd,
    x_ref, dy_ref, rows_ref, sems,
):
    pairs = ((x_hbm, x_ref), (wg_hbm, wg), (wu_hbm, wu), (dy_hbm, dy_ref), (wd_hbm, wd))
    copies = [pltpu.make_async_copy(a, b, sems.at[i]) for i, (a, b) in enumerate(pairs)]
    for copy in copies:
        copy.start()
    copies[0].wait()
    x = x_ref[...]
    gram_x = gram(x)
    copies[1].wait()
    gate_pre = dot(x, wg[...], ((1,), (1,)))
    activated, gelu_slope = gelu_parts(gate_pre)
    copies[2].wait()
    up_pre = dot(x, wu[...], ((1,), (1,)))
    h = (activated * up_pre).astype(BF16)
    copies[3].wait()
    dy = dy_ref[...]
    gram_dy = gram(dy)
    copies[4].wait()
    hidden_grad = dot(dy, wd[...], ((1,), (1,)))
    g = (hidden_grad * up_pre * gelu_slope).astype(BF16)
    u = (hidden_grad * activated).astype(BF16)
    g_ref[...] = g
    u_ref[...] = u
    h_ref[...] = h
    own = jnp.sum(gram_x * (gram(g) + gram(u)) + gram_dy * gram(h))
    total = dot(g, wg[...], ((1,), (0,))) + dot(u, wu[...], ((1,), (0,)))
    rows_ref[...] = total.reshape(rows_ref.shape)
    core = lax.axis_index("core")
    for i in range(NX):
        keep_ref[i] = rows_ref[NC * i + core]
        give_ref[i] = rows_ref[NC * i + 1 - core]
    for ref in (keep_ref, give_ref):
        ref[NX] = jnp.full(ref.shape[1:], own, F32)


def spread_kernel(keep_ref, got_ref, mine_ref, out1, out3, out2, rows_ref):
    rows_ref[...] = keep_ref[...] + got_ref[...]
    x = lax.axis_index("x")
    size = rows_ref.shape[1]
    for step, out_ref in ((0, mine_ref), (1, out1), (3, out3), (2, out2)):
        out_ref[:size, :] = rows_ref[lax.rem(x + step, NX)]
        out_ref[size:, :] = rows_ref[NX, :8, :]


def gather_kernel(mine_ref, got1, got3, got2, later_ref, input_ref, scale_ref, *, factor):
    total = mine_ref[...] + (got1[...] + got3[...]) + got2[...]
    size = input_ref.shape[0]
    input_ref[...] = total[:size].astype(BF16)
    own = total[size:, :128]
    scale_ref[...] = jnp.minimum(1.0, CLIP_NORM / jnp.sqrt(later_ref[0] + own)) * factor


def order_kernel(array_ref, token_ref, out_ref):
    pass


def after(array, token):
    return pl.pallas_call(
        order_kernel,
        out_shape=jax.ShapeDtypeStruct(array.shape, array.dtype),
        in_specs=[pl.BlockSpec(memory_space=pl.ANY)] * 2,
        out_specs=pl.BlockSpec(memory_space=pl.ANY),
        input_output_aliases={0: 0},
        compiler_params=pltpu.CompilerParams(vmem_limit_bytes=1024 * 1024),
        name="order",
    )(array, token)


def merge(got_refs, swap_refs, xs, dys):
    first = lax.axis_index("core") == 0
    row = 0
    for got_ref, swap_ref in zip(got_refs, swap_refs):
        rows = slice(row, row + got_ref.shape[0])
        row += got_ref.shape[0]

        @pl.when(first)
        def _():
            xs[rows, :] = got_ref[...].astype(BF16)
            dys[rows, :] = swap_ref[...].astype(BF16)

        @pl.when(jnp.logical_not(first))
        def _():
            xs[rows, :] = swap_ref[...].astype(BF16)
            dys[rows, :] = got_ref[...].astype(BF16)


def take_part(source_ref, target_ref, offset):
    tokens, width = source_ref.shape
    part = width // NY
    y = lax.axis_index("y")
    for k in range(NY):

        @pl.when(y == k)
        def _():
            target_ref[offset : offset + tokens, :] = source_ref[:, k * part : (k + 1) * part]


def pair_kernel(
    got0, got1, swap0, swap1, wg_ref, wu_ref, wd_ref, g_ref, u_ref, h_ref, xp_ref, dyp_ref, xs, dys
):
    merge((got0, got1), (swap0, swap1), xs, dys)
    take_part(xs, xp_ref, 0)
    take_part(dys, dyp_ref, 0)
    g, u, h = forward(xs[...], dys[...], wg_ref[...], wu_ref[...], wd_ref[...])
    g_ref[...] = g
    u_ref[...] = u
    h_ref[...] = h


def last_kernel(
    scale0, scale1, scale2, scale3, x_ref, dy_ref, g_ref, u_ref, h_ref, g12_ref, u12_ref, h12_ref, xp_ref, dyp_ref,
    got, swap, wg_ref, wu_ref, wd_ref, *refs,
):
    out_refs = refs[: 2 * NZ]
    xs, dys, x_part, dy_part, blocks = refs[2 * NZ :]
    tokens, width = x_ref.shape
    part = width // NY
    merge((got,), (swap,), xs, dys)
    take_part(x_ref, x_part, 0)
    take_part(dy_ref, dy_part, 0)
    take_part(xs, x_part, 3 * tokens)
    take_part(dys, dy_part, 3 * tokens)
    x_part[tokens : 3 * tokens, :] = xp_ref[...]
    dy_part[tokens : 3 * tokens, :] = dyp_ref[...]
    last = forward(xs[...], dys[...], wg_ref[...], wu_ref[...], wd_ref[...])
    rows = part // NZ
    half = blocks.shape[2]
    for m, (left, mine, pair, other) in enumerate(
        (
            (x_part, g_ref, g12_ref, last[0]),
            (x_part, u_ref, u12_ref, last[1]),
            (dy_part, h_ref, h12_ref, last[2]),
        )
    ):
        pieces = (mine[...], pair[:tokens], pair[tokens:], other)
        scaled = [
            (piece.astype(F32) * scale[0:1, 0:1]).astype(BF16)
            for piece, scale in zip(pieces, (scale0, scale1, scale2, scale3))
        ]
        grad = dot(left[...], jnp.concatenate(scaled, axis=0), ((0,), (0,)))
        lo, hi = m * rows, (m + 1) * rows
        for z in range(NZ):
            if lo < half:
                stop = min(hi, half)
                blocks[z, 0, lo:stop, :] = grad[z * rows : z * rows + stop - lo]
            if hi > half:
                start = max(lo, half)
                blocks[z, 1, start - half : hi - half, :] = grad[z * rows + start - lo : (z + 1) * rows]
    me = lax.axis_index("z")
    for z in range(NZ):
        owner = lax.rem(me + z, NZ)
        for i in range(2):
            out_refs[2 * z + i][...] = blocks[owner, i]


def add_kernel(a_ref, b_ref, out_ref):
    out_ref[...] = a_ref[...] + b_ref[...]


def finish_kernel(top0, top1, top2, low0, low1, low2, gate_ref, up_ref, down_ref):
    rows = gate_ref.shape[0]
    half = top0.shape[0]
    top = top0[...] + (top1[...] + top2[...])
    low = low0[...] + (low1[...] + low2[...])
    gate_ref[...] = top[:rows]
    up_ref[: half - rows, :] = top[rows:]
    up_ref[half - rows :, :] = low[: 2 * rows - half]
    down_ref[...] = low[2 * rows - half : 3 * rows - half]


def per_device(inputs, gate_weight, up_weight, down_weight, out_grad, later_norms):
    tokens, width = inputs.shape
    ff = gate_weight.shape[1]
    part = width // NY
    rows = part // NZ
    half_rows = -(-3 * rows // 16) * 8
    slice_rows = tokens // (NX * NC)
    weights = (gate_weight.T, up_weight.T, down_weight.T)

    def shape(*dims, dtype=F32):
        return jax.ShapeDtypeStruct(dims, dtype)

    def call(kernel, name, outs, scratch, macs, mib, *args, spaces=()):
        spaces = dict(spaces)
        vmem = pl.BlockSpec(memory_space=pltpu.VMEM)
        return pl.pallas_call(
            kernel,
            out_shape=outs,
            in_specs=[pl.BlockSpec(memory_space=spaces.get(i, pltpu.VMEM)) for i in range(len(args))],
            out_specs=jax.tree.map(lambda _: vmem, outs),
            scratch_shapes=scratch,
            compiler_params=pltpu.CompilerParams(vmem_limit_bytes=mib * 1024 * 1024),
            cost_estimate=pl.CostEstimate(
                flops=macs * 4 * tokens * width * ff,
                bytes_accessed=sum(a.size * a.dtype.itemsize for a in args) if macs else 0,
                transcendentals=0,
            ),
            name=name,
        )(*args)

    mine, token = call(
        prepare_kernel, "prepare", [shape(tokens, width), shape(8, 128)], [], 0, 4, inputs, out_grad
    )
    got = [shift(mine, "y", k) for k in (1, 3, 2)]

    hiddens = [shape(tokens, ff, dtype=BF16)] * 3
    group = shape(NX + 1, slice_rows, width)
    *own_back, keep, give, wg, wu, wd = call(
        own_kernel, "own_example", hiddens + [group] * 2 + [shape(ff, width, dtype=BF16)] * 3,
        [pltpu.VMEM((tokens, width), BF16)] * 2
        + [pltpu.VMEM((NX * NC, slice_rows, width), F32), pltpu.SemaphoreType.DMA((5,))],
        0, OWN_MIB, inputs, out_grad, *weights, shift(token, "core", 1),
        spaces=[(i, pl.ANY) for i in range(6)],
    )
    weights = (wg, wu, wd)
    one = shape(slice_rows + 8, width)
    first, *rest = call(
        spread_kernel, "input_spread", [one] * 4, [pltpu.VMEM(group.shape, F32)], 0, 4,
        keep, shift(give, "core", 1),
    )
    rest = [shift(a, "x", k) for a, k in zip(rest, (1, 3, 2))]
    input_grad, scale = call(
        functools.partial(gather_kernel, factor=math.sqrt(width * ff * NX * NC / (NY * NZ))),
        "input_sum", [shape(slice_rows, width, dtype=BF16), shape(8, 128)], [], 0, 2,
        first, *rest, later_norms,
        spaces=[(4, pltpu.SMEM)],
    )
    scales = [scale] + [shift(scale, "y", k) for k in (1, 3, 2)]

    got = [after(a, t) for a, t in zip(got, (rest[2], rest[2], scale))]
    swapped = [shift(a, "core", 1) for a in got]
    both = [shape(2 * tokens, ff, dtype=BF16)] * 3 + [shape(2 * tokens, part, dtype=BF16)] * 2
    pair_back = call(
        pair_kernel, "pair_examples", both, [pltpu.VMEM((2 * tokens, width), BF16)] * 2, 6, 16,
        *got[:2], *swapped[:2], *weights,
    )
    blocks = call(
        last_kernel, "group_gradients", [shape(half_rows, ff)] * (2 * NZ),
        [pltpu.VMEM((tokens, width), BF16)] * 2 + [pltpu.VMEM((NY * tokens, part), BF16)] * 2
        + [pltpu.VMEM((NZ, 2, half_rows, ff), F32)], 6, 20,
        *scales, inputs, out_grad, *own_back, *pair_back, got[2], swapped[2], *weights,
    )
    plan = ((0, 1, 4), (1, -1, 4), (1, 1, 3), (0, -1, 3))
    held = [blocks[2 * (d * n % NZ) + i] for i, d, n in plan]
    for step in range(4):
        for c, (i, d, n) in enumerate(plan):
            if step < n:
                held[c] = shift(held[c], "z", d)
                if step < n - 1:
                    held[c] = call(
                        add_kernel, "add_block", shape(half_rows, ff), [], 0, 4,
                        held[c], blocks[2 * (d * (n - 1 - step) % NZ) + i],
                    )
    grads = call(
        finish_kernel, "finish", [shape(rows, ff)] * 3, [], 0, 4,
        blocks[0], held[0], held[3], blocks[1], held[1], held[2],
    )
    return (input_grad, *grads)


def solution(mesh):
    fine = Mesh(mesh.devices.reshape(NY, NZ, NX, NC), ("y", "z", "x", "core"))
    dp, tensor = ("y", "z"), ("x", "core")
    in_specs = (
        P(dp, None),
        P(None, tensor),
        P(None, tensor),
        P(None, tensor),
        P(dp, None),
        P(dp),
    )
    out_specs = (P(dp + tensor, None), P(dp, tensor), P(dp, tensor), P(dp, tensor))
    return jax.shard_map(
        per_device, mesh=fine, in_specs=in_specs, out_specs=out_specs, check_vma=False
    )
```

time: 315 us -> 89.9 us (0.29)
  waiting for transfers between devices: 255 us -> 26.3 us
  starting transfers between devices: 0.08 us -> 43.4 us
  between operations: 17.6 us -> 1.46 us
  matrix products: 15.6 us -> 0 us
  blocking collectives: 15.2 us -> 0 us
  Pallas kernels: 0 us -> 14.5 us
  local copies, waits for them, and re-layouts: 7.86 us -> 3.84 us
    unnamed x3 -> x0, waiting for transfers between devices: 248 us -> none
    ppermute x0 -> x28, starting transfers between devices: none -> 43.4 us  [shift(): lax.ppermute(array, axis, [(i, (i + step) % size) for i in range(size)])]
    ppermute x0 -> x28, waiting for transfers between devices: none -> 26.3 us  [shift(): lax.ppermute(array, axis, [(i, (i + step) % size) for i in range(size)])]
    dot_general x13 -> x0, matrix products: 15.6 us -> none  [the longest x3 7.83 us: token_products(): lax.dot_general(left, right, (((0,), (0,)), ((), ())), preferred_element_...]
    psum x1 -> x0, blocking collectives: 15.2 us -> none  [per_device(): own_norm = lax.psum(own_part, 'tensor')]
    pallas_call x0 -> x20, Pallas kernels: none -> 14.5 us  [the longest x17 14.5 us: call(): pl.pallas_call(kernel, out_shape=outs, in_specs=[pl.BlockSpec(memory_spac...]
    reduce_scatter x1 -> x0, waiting for transfers between devices: 7.37 us -> none  [per_device(): lax.psum_scatter(lax.dot_general(gate_back, gate_weight, feature_contract...]
    unnamed x18 -> x10, local copies, waits for them, and re-layouts: 7.86 us -> 3.84 us
  transfers between devices with their start and end apart: 2 -> 28, of which waited for: 2 -> 13; matrix products, arithmetic and copies ran while one was open for 4% -> 0% of each run, Pallas kernels for 0% -> 11%
where the time goes in v2:
time: 89.9 us; the launch traced here: 89.5 us
  starting transfers between devices  43.4 us (48%)
  waiting for transfers between devices  26.3 us (29%)
  Pallas kernels  14.5 us (16%)
  local copies, waits for them, and re-layouts  3.84 us (4%)
  between operations  1.46 us (2%)
    ppermute x28, starting transfers between devices, shift(): lax.ppermute(array, axis, [(i, (i + step) % size) for i in range(size)])  43.4 us
    ppermute x28, waiting for transfers between devices, shift(): lax.ppermute(array, axis, [(i, (i + step) % size) for i in range(size)])  26.3 us
    pallas_call x17, Pallas kernels, call(): pl.pallas_call(kernel, out_shape=outs, in_specs=[pl.BlockSpec(memory_spac...  14.5 us
    unnamed x10, local copies, waits for them, and re-layouts  3.84 us
  transfers between devices with their start and end apart: 28, of which 13 were waited for; matrix products, arithmetic and copies ran while one was open for 0% of the time, Pallas kernels for 11%

profile of v2, /device:TPU:96, one launch (start us, length us, event | category | flops | bytes accessed | tf_op | source)
XLA Modules:
  0.0 89.5 jit_solution(8286427287515018907)
XLA Ops:
  0.6 0.0 copy-start
  0.6 1.0 %copy-done = bf16[128,1152]{1,0:T(8,128)(2,1)S(1)} copy-done((bf16[128,1152]{1,0:T(8,128)(2,1)S(1)}, bf16[128,1152]{1,0:T(8,128)(2,1)}, u32[]{:S(2)}) %copy-start) | copy-done | bytes 294936
  1.6 1.0 %copy-done.2 = bf16[128,1152]{1,0:T(8,128)(2,1)S(1)} copy-done((bf16[128,1152]{1,0:T(8,128)(2,1)S(1)}, bf16[128,1152]{1,0:T(8,128)(2,1)}, u32[]{:S(2)}) %copy-start.2) | copy-done | bytes 294936
  2.6 1.7 %collective-permute-start.8 = (f32[128,1152]{1,0:T(8,128)S(1)}, f32[128,1152]{1,0:T(8,128)S(1)}, u32[]{:S(2)}, u32[]{:S(2)}) collective-permute-start(f32[128,1152]{1,0:T(8,128)S(1)} %get-tuple-element.56), channel_id=1, source_target_pairs={{0,64},{64,128},{128,192},{192,0},{1,65},{65,129},{129,193},{193,1... | collective-permute-start | bytes 1769480 | tf_op jit(solution)/shard_map/ppermute | solution.py:30
  4.3 1.7 %collective-permute-start.9 = (f32[128,1152]{1,0:T(8,128)S(1)}, f32[128,1152]{1,0:T(8,128)S(1)}, u32[]{:S(2)}, u32[]{:S(2)}) collective-permute-start(f32[128,1152]{1,0:T(8,128)S(1)} %get-tuple-element.56), channel_id=1, source_target_pairs={{0,192},{64,0},{128,64},{192,128},{1,193},{65,1},{129,65},{193,129... | collective-permute-start | bytes 1769480 | tf_op jit(solution)/shard_map/ppermute | solution.py:30
  5.9 0.0 collective-permute-start
  5.9 1.2 %collective-permute-done.token_ref = f32[8,128]{1,0:T(8,128)S(1)} collective-permute-done((f32[8,128]{1,0:T(8,128)S(1)}, f32[8,128]{1,0:T(8,128)S(1)}, u32[]{:S(2)}, u32[]{:S(2)}) %collective-permute-start) | collective-permute-done | bytes 4128 | tf_op jit(solution)/shard_map/ppermute | solution.py:30
  7.1 1.0 %copy-done.1 = bf16[128,1152]{1,0:T(8,128)(2,1)S(1)} copy-done((bf16[128,1152]{1,0:T(8,128)(2,1)S(1)}, bf16[128,1152]{1,0:T(8,128)(2,1)}, u32[]{:S(2)}) %copy-start.1) | copy-done | bytes 294936
  8.1 1.0 %copy-done.3 = bf16[128,1152]{1,0:T(8,128)(2,1)S(1)} copy-done((bf16[128,1152]{1,0:T(8,128)(2,1)S(1)}, bf16[128,1152]{1,0:T(8,128)(2,1)}, u32[]{:S(2)}) %copy-start.3) | copy-done | bytes 294936
  9.0 6.4 %own_example.1 = (bf16[128,864]{1,0:T(8,128)(2,1)S(1)}, bf16[128,864]{1,0:T(8,128)(2,1)S(1)}, bf16[128,864]{1,0:T(8,128)(2,1)S(1)}, f32[5,16,1152]{2,1,0:T(8,128...) custom-call(bf16[128,1152]{1,0:T(8,128)(2,1)S(1)} %copy-done.1, ...), custom_call_target="tpu_custom_call" | custom-call | tf_op jit(solution)/shard_map/own_example/pallas_call | solution.py:253
  15.4 0.3 collective-permute-start.1
  15.7 2.0 %collective-permute-start.12 = (f32[128,1152]{1,0:T(8,128)S(1)}, f32[128,1152]{1,0:T(8,128)S(1)}, u32[]{:S(2)}, u32[]{:S(2)}) collective-permute-start(f32[128,1152]{1,0:T(8,128)S(1)} %get-tuple-element.56), channel_id=1, source_target_pairs={{0,128},{64,192},{128,0},{192,64},{1,129},{65,193},{129,1},{193,65... | collective-permute-start | bytes 1769480 | tf_op jit(solution)/shard_map/ppermute | solution.py:30
  17.7 0.0 collective-permute-done.1.got_ref
  17.7 0.1 input_spread.1
  17.8 3.1 %collective-permute-start.4 = (f32[24,1152]{1,0:T(8,128)S(1)}, f32[24,1152]{1,0:T(8,128)S(1)}, u32[]{:S(2)}, u32[]{:S(2)}) collective-permute-start(f32[24,1152]{1,0:T(8,128)S(1)} %get-tuple-element.50), channel_id=1, source_target_pairs={{0,4},{2,6},{4,0},{6,2},{1,5},{3,7},{5,1},{7,3},{8,12},{10,14},{12... | collective-permute-start | bytes 331784 | tf_op jit(solution)/shard_map/ppermute | solution.py:30
  20.9 3.5 %collective-permute-done.4.got2.token_ref = f32[24,1152]{1,0:T(8,128)S(1)} collective-permute-done((f32[24,1152]{1,0:T(8,128)S(1)}, f32[24,1152]{1,0:T(8,128)S(1)}, u32[]{:S(2)}, u32[]{:S(2)}) %collective-permute-start.4) | collective-permute-done | bytes 110624 | tf_op jit(solution)/shard_map/ppermute | solution.py:30
  24.4 0.0 collective-permute-done.8.array_ref
  24.4 0.0 collective-permute-start.10
  24.4 0.0 collective-permute-done.9.array_ref
  24.4 0.5 collective-permute-start.11
  24.9 1.5 %collective-permute-start.2 = (f32[24,1152]{1,0:T(8,128)S(1)}, f32[24,1152]{1,0:T(8,128)S(1)}, u32[]{:S(2)}, u32[]{:S(2)}) collective-permute-start(f32[24,1152]{1,0:T(8,128)S(1)} %get-tuple-element.48), channel_id=1, source_target_pairs={{0,2},{2,4},{4,6},{6,0},{1,3},{3,5},{5,7},{7,1},{8,10},{10,12},{12... | collective-permute-start | bytes 331784 | tf_op jit(solution)/shard_map/ppermute | solution.py:30
  26.4 1.7 %collective-permute-start.3 = (f32[24,1152]{1,0:T(8,128)S(1)}, f32[24,1152]{1,0:T(8,128)S(1)}, u32[]{:S(2)}, u32[]{:S(2)}) collective-permute-start(f32[24,1152]{1,0:T(8,128)S(1)} %get-tuple-element.49), channel_id=1, source_target_pairs={{0,6},{2,0},{4,2},{6,4},{1,7},{3,1},{5,3},{7,5},{8,14},{10,8},{12,... | collective-permute-start | bytes 331784 | tf_op jit(solution)/shard_map/ppermute | solution.py:30
  28.8 2.4 %collective-permute-done.2.got1 = f32[24,1152]{1,0:T(8,128)S(1)} collective-permute-done((f32[24,1152]{1,0:T(8,128)S(1)}, f32[24,1152]{1,0:T(8,128)S(1)}, u32[]{:S(2)}, u32[]{:S(2)}) %collective-permute-start.2) | collective-permute-done | bytes 110624 | tf_op jit(solution)/shard_map/ppermute | solution.py:30
  31.2 0.0 collective-permute-done.3.got3
  31.2 0.6 input_sum.1
  31.8 1.0 %collective-permute-done.12.array_ref = f32[128,1152]{1,0:T(8,128)S(1)} collective-permute-done((f32[128,1152]{1,0:T(8,128)S(1)}, f32[128,1152]{1,0:T(8,128)S(1)}, u32[]{:S(2)}, u32[]{:S(2)}) %collective-permute-start.12) | collective-permute-done | bytes 589856 | tf_op jit(solution)/shard_map/ppermute | solution.py:30
  32.8 0.0 collective-permute-start.13
  32.8 1.9 %collective-permute-start.7 = (f32[8,128]{1,0:T(8,128)S(1)}, f32[8,128]{1,0:T(8,128)S(1)}, u32[]{:S(2)}, u32[]{:S(2)}) collective-permute-start(f32[8,128]{1,0:T(8,128)S(1)} %get-tuple-element.52.token_ref.scale0), channel_id=1, source_target_pairs={{0,128},{64,192},{128,0},{192,64},{1,129},{65,193},{129,1},{193,65... | collective-permute-start | bytes 12296 | tf_op jit(solution)/shard_map/ppermute | solution.py:30
  34.8 7.4 %collective-permute-start.6 = (f32[8,128]{1,0:T(8,128)S(1)}, f32[8,128]{1,0:T(8,128)S(1)}, u32[]{:S(2)}, u32[]{:S(2)}) collective-permute-start(f32[8,128]{1,0:T(8,128)S(1)} %get-tuple-element.52.token_ref.scale0), channel_id=1, source_target_pairs={{0,192},{64,0},{128,64},{192,128},{1,193},{65,1},{129,65},{193,129... | collective-permute-start | bytes 12296 | tf_op jit(solution)/shard_map/ppermute | solution.py:30
  42.1 0.0 collective-permute-done.10.swap0
  42.1 0.8 collective-permute-start.5
  42.9 0.0 collective-permute-done.11.swap1
  42.9 2.8 %pair_examples.1 = (bf16[256,864]{1,0:T(8,128)(2,1)S(1)}, bf16[256,864]{1,0:T(8,128)(2,1)S(1)}, bf16[256,864]{1,0:T(8,128)(2,1)S(1)}, bf16[256,288]{1,0:T(8,128)(2,1)S(1)}, bf16[256,288]{1,0:T(8,128)(2,1)S(1)}) custom-call(f32[128,1152]{1,0:T(8,128)S(1)} %order.3.got0, f32[128,1152]{1,0:T(8,128)S(1)} %order.4.got1, ...), custom_call_target="tpu_custom_call" | custom-call | flops 3057647616 | bytes 8331264 | tf_op jit(solution)/shard_map/pair_examples/pallas_call | solution.py:253
  45.7 0.0 collective-permute-done.7.scale3
  45.7 0.0 collective-permute-done.6.scale2
  45.7 1.2 %collective-permute-done.5.scale1 = f32[8,128]{1,0:T(8,128)S(1)} collective-permute-done((f32[8,128]{1,0:T(8,128)S(1)}, f32[8,128]{1,0:T(8,128)S(1)}, u32[]{:S(2)}, u32[]{:S(2)}) %collective-permute-start.5) | collective-permute-done | bytes 4128 | tf_op jit(solution)/shard_map/ppermute | solution.py:30
  46.9 0.0 collective-permute-done.13.swap
  47.0 3.5 %group_gradients.1 = (f32[56,864]{1,0:T(8,128)S(1)}, f32[56,864]{1,0:T(8,128)S(1)}, f32[56,864]{1,0:T(8,128)S(1)}, f32[56,864]{1,0:T(8,128)S(1)}, f32[56,864]{1,...) custom-call(f32[8,128]{1,0:T(8,128)S(1)} %get-tuple-element.52.token, ...), custom_call_target="tpu_custom_call" | custom-call | flops 3057647616 | bytes 10043392 | tf_op jit(solution)/shard_map/group_gradients/pallas_call | solution.py:253
  50.4 3.2 %collective-permute-start.14 = (f32[56,864]{1,0:T(8,128)S(1)}, f32[56,864]{1,0:T(8,128)S(1)}, u32[]{:S(2)}, u32[]{:S(2)}) collective-permute-start(f32[56,864]{1,0:T(8,128)S(1)} %get-tuple-element.66), channel_id=1, source_target_pairs={{0,8},{8,16},{16,24},{24,32},{32,40},{40,48},{48,56},{56,0},{1,9},... | collective-permute-start | bytes 580616 | tf_op jit(solution)/shard_map/ppermute | solution.py:30
  53.6 0.0 collective-permute-start.21
  53.6 3.3 %collective-permute-start.25 = (f32[56,864]{1,0:T(8,128)S(1)}, f32[56,864]{1,0:T(8,128)S(1)}, u32[]{:S(2)}, u32[]{:S(2)}) collective-permute-start(f32[56,864]{1,0:T(8,128)S(1)} %get-tuple-element.78), channel_id=1, source_target_pairs={{0,8},{8,16},{16,24},{24,32},{32,40},{40,48},{48,56},{56,0},{1,9},... | collective-permute-start | bytes 580616 | tf_op jit(solution)/shard_map/ppermute | solution.py:30
  56.9 1.8 %collective-permute-done.14.a_ref = f32[56,864]{1,0:T(8,128)S(1)} collective-permute-done((f32[56,864]{1,0:T(8,128)S(1)}, f32[56,864]{1,0:T(8,128)S(1)}, u32[]{:S(2)}, u32[]{:S(2)}) %collective-permute-start.14) | collective-permute-done | bytes 193568 | tf_op jit(solution)/shard_map/ppermute | solution.py:30
  58.7 3.8 %collective-permute-start.15 = (f32[56,864]{1,0:T(8,128)S(1)}, f32[56,864]{1,0:T(8,128)S(1)}, u32[]{:S(2)}, u32[]{:S(2)}) collective-permute-start(f32[56,864]{1,0:T(8,128)S(1)} %add_block.10), channel_id=1, source_target_pairs={{0,8},{8,16},{16,24},{24,32},{32,40},{40,48},{48,56},{56,0},{1,9},... | collective-permute-start | bytes 580616 | tf_op jit(solution)/shard_map/ppermute | solution.py:30
  62.5 0.1 collective-permute-done.21.a_ref
  62.6 0.1 collective-permute-start.22
  62.7 4.2 %collective-permute-done.18.a_ref = f32[56,864]{1,0:T(8,128)S(1)} collective-permute-done((f32[56,864]{1,0:T(8,128)S(1)}, f32[56,864]{1,0:T(8,128)S(1)}, u32[]{:S(2)}, u32[]{:S(2)}) %collective-permute-start.18) | collective-permute-done | bytes 193568 | tf_op jit(solution)/shard_map/ppermute | solution.py:30
  66.9 0.1 collective-permute-start.19
  67.0 3.5 %collective-permute-start.26 = (f32[56,864]{1,0:T(8,128)S(1)}, f32[56,864]{1,0:T(8,128)S(1)}, u32[]{:S(2)}, u32[]{:S(2)}) collective-permute-start(f32[56,864]{1,0:T(8,128)S(1)} %add_block.18), channel_id=1, source_target_pairs={{0,8},{8,16},{16,24},{24,32},{32,40},{40,48},{48,56},{56,0},{1,9},... | collective-permute-start | bytes 580616 | tf_op jit(solution)/shard_map/ppermute | solution.py:30
  70.6 0.1 collective-permute-start.16
  70.7 0.8 collective-permute-done.22.a_ref
  71.5 1.3 %collective-permute-start.23 = (f32[56,864]{1,0:T(8,128)S(1)}, f32[56,864]{1,0:T(8,128)S(1)}, u32[]{:S(2)}, u32[]{:S(2)}) collective-permute-start(f32[56,864]{1,0:T(8,128)S(1)} %add_block.16), channel_id=1, source_target_pairs={{0,56},{8,0},{16,8},{24,16},{32,24},{40,32},{48,40},{56,48},{1,57}... | collective-permute-start | bytes 580616 | tf_op jit(solution)/shard_map/ppermute | solution.py:30
  72.8 3.2 %collective-permute-done.19.a_ref = f32[56,864]{1,0:T(8,128)S(1)} collective-permute-done((f32[56,864]{1,0:T(8,128)S(1)}, f32[56,864]{1,0:T(8,128)S(1)}, u32[]{:S(2)}, u32[]{:S(2)}) %collective-permute-start.19) | collective-permute-done | bytes 193568 | tf_op jit(solution)/shard_map/ppermute | solution.py:30
  76.1 0.1 collective-permute-start.20
  76.2 0.0 collective-permute-done.26.a_ref
  76.2 3.3 %collective-permute-start.27 = (f32[56,864]{1,0:T(8,128)S(1)}, f32[56,864]{1,0:T(8,128)S(1)}, u32[]{:S(2)}, u32[]{:S(2)}) collective-permute-start(f32[56,864]{1,0:T(8,128)S(1)} %add_block.19), channel_id=1, source_target_pairs={{0,8},{8,16},{16,24},{24,32},{32,40},{40,48},{48,56},{56,0},{1,9},... | collective-permute-start | bytes 580616 | tf_op jit(solution)/shard_map/ppermute | solution.py:30
  79.5 0.0 collective-permute-done.16.a_ref
  79.5 2.1 %collective-permute-start.17 = (f32[56,864]{1,0:T(8,128)S(1)}, f32[56,864]{1,0:T(8,128)S(1)}, u32[]{:S(2)}, u32[]{:S(2)}) collective-permute-start(f32[56,864]{1,0:T(8,128)S(1)} %add_block.12), channel_id=1, source_target_pairs={{0,8},{8,16},{16,24},{24,32},{32,40},{40,48},{48,56},{56,0},{1,9},... | collective-permute-start | bytes 580616 | tf_op jit(solution)/shard_map/ppermute | solution.py:30
  81.6 0.0 collective-permute-done.23.a_ref
  81.7 0.1 collective-permute-start.24
  81.8 2.3 %collective-permute-done.20.top2 = f32[56,864]{1,0:T(8,128)S(1)} collective-permute-done((f32[56,864]{1,0:T(8,128)S(1)}, f32[56,864]{1,0:T(8,128)S(1)}, u32[]{:S(2)}, u32[]{:S(2)}) %collective-permute-start.20) | collective-permute-done | bytes 193568 | tf_op jit(solution)/shard_map/ppermute | solution.py:30
  84.1 0.0 collective-permute-done.27.low2
  84.1 1.2 %collective-permute-done.17.top1 = f32[56,864]{1,0:T(8,128)S(1)} collective-permute-done((f32[56,864]{1,0:T(8,128)S(1)}, f32[56,864]{1,0:T(8,128)S(1)}, u32[]{:S(2)}, u32[]{:S(2)}) %collective-permute-start.17) | collective-permute-done | bytes 193568 | tf_op jit(solution)/shard_map/ppermute | solution.py:30
  85.3 3.4 %collective-permute-done.24.low1 = f32[56,864]{1,0:T(8,128)S(1)} collective-permute-done((f32[56,864]{1,0:T(8,128)S(1)}, f32[56,864]{1,0:T(8,128)S(1)}, u32[]{:S(2)}, u32[]{:S(2)}) %collective-permute-start.24) | collective-permute-done | bytes 193568 | tf_op jit(solution)/shard_map/ppermute | solution.py:30
  88.7 0.8 finish.1
  (22 shorter events, 0.3 us)
Async XLA Ops:
  0.6 1.0 %copy-start = (bf16[128,1152]{1,0:T(8,128)(2,1)S(1)}, bf16[128,1152]{1,0:T(8,128)(2,1)}, u32[]{:S(2)}) copy-start(bf16[128,1152]{1,0:T(8,128)(2,1)} %x_ref.3) | copy-start | bytes 884740
  1.6 1.0 %copy-start.2 = (bf16[128,1152]{1,0:T(8,128)(2,1)S(1)}, bf16[128,1152]{1,0:T(8,128)(2,1)}, u32[]{:S(2)}) copy-start(bf16[128,1152]{1,0:T(8,128)(2,1)} %dy_ref.3) | copy-start | bytes 884740
  2.6 21.8 %collective-permute-start.8 = (f32[128,1152]{1,0:T(8,128)S(1)}, f32[128,1152]{1,0:T(8,128)S(1)}, u32[]{:S(2)}, u32[]{:S(2)}) collective-permute-start(f32[128,1152]{1,0:T(8,128)S(1)} %get-tuple-element.56), channel_id=1, source_target_pairs={{0,64},{64,128},{128,192},{192,0},{1,65},{65,129},{129,193},{193,1... | collective-permute-start | bytes 1769480 | tf_op jit(solution)/shard_map/ppermute | solution.py:30
  4.3 20.1 %collective-permute-start.9 = (f32[128,1152]{1,0:T(8,128)S(1)}, f32[128,1152]{1,0:T(8,128)S(1)}, u32[]{:S(2)}, u32[]{:S(2)}) collective-permute-start(f32[128,1152]{1,0:T(8,128)S(1)} %get-tuple-element.56), channel_id=1, source_target_pairs={{0,192},{64,0},{128,64},{192,128},{1,193},{65,1},{129,65},{193,129... | collective-permute-start | bytes 1769480 | tf_op jit(solution)/shard_map/ppermute | solution.py:30
  5.9 1.2 %collective-permute-start = (f32[8,128]{1,0:T(8,128)S(1)}, f32[8,128]{1,0:T(8,128)S(1)}, u32[]{:S(2)}, u32[]{:S(2)}) collective-permute-start(f32[8,128]{1,0:T(8,128)S(1)} %get-tuple-element.44), channel_id=1, source_target_pairs={{0,1},{1,0},{2,3},{3,2},{4,5},{5,4},{6,7},{7,6},{8,9},{9,8},{10,11... | collective-permute-start | bytes 12296 | tf_op jit(solution)/shard_map/ppermute | solution.py:30
  7.1 1.0 %copy-start.1 = (bf16[128,1152]{1,0:T(8,128)(2,1)S(1)}, bf16[128,1152]{1,0:T(8,128)(2,1)}, u32[]{:S(2)}) copy-start(bf16[128,1152]{1,0:T(8,128)(2,1)} %x_ref.3) | copy-start | bytes 884740
  8.1 1.0 %copy-start.3 = (bf16[128,1152]{1,0:T(8,128)(2,1)S(1)}, bf16[128,1152]{1,0:T(8,128)(2,1)}, u32[]{:S(2)}) copy-start(bf16[128,1152]{1,0:T(8,128)(2,1)} %dy_ref.3) | copy-start | bytes 884740
  15.4 2.2 %collective-permute-start.1 = (f32[5,16,1152]{2,1,0:T(8,128)S(1)}, f32[5,16,1152]{2,1,0:T(8,128)S(1)}, u32[]{:S(2)}, u32[]{:S(2)}) collective-permute-start(f32[5,16,1152]{2,1,0:T(8,128)S(1)} %get-tuple-element.46), channel_id=1, source_target_pairs={{0,1},{1,0},{2,3},{3,2},{4,5},{5,4},{6,7},{7,6},{8,9},{9,8},{10,11... | collective-permute-start | bytes 1105928 | tf_op jit(solution)/shard_map/ppermute | solution.py:30
  15.7 17.1 %collective-permute-start.12 = (f32[128,1152]{1,0:T(8,128)S(1)}, f32[128,1152]{1,0:T(8,128)S(1)}, u32[]{:S(2)}, u32[]{:S(2)}) collective-permute-start(f32[128,1152]{1,0:T(8,128)S(1)} %get-tuple-element.56), channel_id=1, source_target_pairs={{0,128},{64,192},{128,0},{192,64},{1,129},{65,193},{129,1},{193,65... | collective-permute-start | bytes 1769480 | tf_op jit(solution)/shard_map/ppermute | solution.py:30
  17.8 25.2 %copy-start.4 = (bf16[864,1152]{1,0:T(8,128)(2,1)S(1)}, bf16[864,1152]{1,0:T(8,128)(2,1)}, u32[]{:S(2)}) copy-start(bf16[864,1152]{1,0:T(8,128)(2,1)} %get-tuple-element.59.wd_ref) | copy-start | bytes 5971972
  17.8 6.6 %collective-permute-start.4 = (f32[24,1152]{1,0:T(8,128)S(1)}, f32[24,1152]{1,0:T(8,128)S(1)}, u32[]{:S(2)}, u32[]{:S(2)}) collective-permute-start(f32[24,1152]{1,0:T(8,128)S(1)} %get-tuple-element.50), channel_id=1, source_target_pairs={{0,4},{2,6},{4,0},{6,2},{1,5},{3,7},{5,1},{7,3},{8,12},{10,14},{12... | collective-permute-start | bytes 331784 | tf_op jit(solution)/shard_map/ppermute | solution.py:30
  24.4 17.7 %collective-permute-start.10 = (f32[128,1152]{1,0:T(8,128)S(1)}, f32[128,1152]{1,0:T(8,128)S(1)}, u32[]{:S(2)}, u32[]{:S(2)}) collective-permute-start(f32[128,1152]{1,0:T(8,128)S(1)} %order.3.got0), channel_id=1, source_target_pairs={{0,1},{1,0},{2,3},{3,2},{4,5},{5,4},{6,7},{7,6},{8,9},{9,8},{10,11... | collective-permute-start | bytes 1769480 | tf_op jit(solution)/shard_map/ppermute | solution.py:30
  24.4 18.5 %collective-permute-start.11 = (f32[128,1152]{1,0:T(8,128)S(1)}, f32[128,1152]{1,0:T(8,128)S(1)}, u32[]{:S(2)}, u32[]{:S(2)}) collective-permute-start(f32[128,1152]{1,0:T(8,128)S(1)} %order.4.got1), channel_id=1, source_target_pairs={{0,1},{1,0},{2,3},{3,2},{4,5},{5,4},{6,7},{7,6},{8,9},{9,8},{10,11... | collective-permute-start | bytes 1769480 | tf_op jit(solution)/shard_map/ppermute | solution.py:30
  24.9 6.3 %collective-permute-start.2 = (f32[24,1152]{1,0:T(8,128)S(1)}, f32[24,1152]{1,0:T(8,128)S(1)}, u32[]{:S(2)}, u32[]{:S(2)}) collective-permute-start(f32[24,1152]{1,0:T(8,128)S(1)} %get-tuple-element.48), channel_id=1, source_target_pairs={{0,2},{2,4},{4,6},{6,0},{1,3},{3,5},{5,7},{7,1},{8,10},{10,12},{12... | collective-permute-start | bytes 331784 | tf_op jit(solution)/shard_map/ppermute | solution.py:30
  26.4 4.8 %collective-permute-start.3 = (f32[24,1152]{1,0:T(8,128)S(1)}, f32[24,1152]{1,0:T(8,128)S(1)}, u32[]{:S(2)}, u32[]{:S(2)}) collective-permute-start(f32[24,1152]{1,0:T(8,128)S(1)} %get-tuple-element.49), channel_id=1, source_target_pairs={{0,6},{2,0},{4,2},{6,4},{1,7},{3,1},{5,3},{7,5},{8,14},{10,8},{12,... | collective-permute-start | bytes 331784 | tf_op jit(solution)/shard_map/ppermute | solution.py:30
  32.8 14.1 %collective-permute-start.13 = (f32[128,1152]{1,0:T(8,128)S(1)}, f32[128,1152]{1,0:T(8,128)S(1)}, u32[]{:S(2)}, u32[]{:S(2)}) collective-permute-start(f32[128,1152]{1,0:T(8,128)S(1)} %order.5.got), channel_id=1, source_target_pairs={{0,1},{1,0},{2,3},{3,2},{4,5},{5,4},{6,7},{7,6},{8,9},{9,8},{10,11... | collective-permute-start | bytes 1769480 | tf_op jit(solution)/shard_map/ppermute | solution.py:30
  32.8 12.9 %collective-permute-start.7 = (f32[8,128]{1,0:T(8,128)S(1)}, f32[8,128]{1,0:T(8,128)S(1)}, u32[]{:S(2)}, u32[]{:S(2)}) collective-permute-start(f32[8,128]{1,0:T(8,128)S(1)} %get-tuple-element.52.token_ref.scale0), channel_id=1, source_target_pairs={{0,128},{64,192},{128,0},{192,64},{1,129},{65,193},{129,1},{193,65... | collective-permute-start | bytes 12296 | tf_op jit(solution)/shard_map/ppermute | solution.py:30
  34.8 11.0 %collective-permute-start.6 = (f32[8,128]{1,0:T(8,128)S(1)}, f32[8,128]{1,0:T(8,128)S(1)}, u32[]{:S(2)}, u32[]{:S(2)}) collective-permute-start(f32[8,128]{1,0:T(8,128)S(1)} %get-tuple-element.52.token_ref.scale0), channel_id=1, source_target_pairs={{0,192},{64,0},{128,64},{192,128},{1,193},{65,1},{129,65},{193,129... | collective-permute-start | bytes 12296 | tf_op jit(solution)/shard_map/ppermute | solution.py:30
  42.1 4.8 %collective-permute-start.5 = (f32[8,128]{1,0:T(8,128)S(1)}, f32[8,128]{1,0:T(8,128)S(1)}, u32[]{:S(2)}, u32[]{:S(2)}) collective-permute-start(f32[8,128]{1,0:T(8,128)S(1)} %get-tuple-element.52.token_ref.scale0), channel_id=1, source_target_pairs={{0,64},{64,128},{128,192},{192,0},{1,65},{65,129},{129,193},{193,1... | collective-permute-start | bytes 12296 | tf_op jit(solution)/shard_map/ppermute | solution.py:30
  50.4 8.3 %collective-permute-start.14 = (f32[56,864]{1,0:T(8,128)S(1)}, f32[56,864]{1,0:T(8,128)S(1)}, u32[]{:S(2)}, u32[]{:S(2)}) collective-permute-start(f32[56,864]{1,0:T(8,128)S(1)} %get-tuple-element.66), channel_id=1, source_target_pairs={{0,8},{8,16},{16,24},{24,32},{32,40},{40,48},{48,56},{56,0},{1,9},... | collective-permute-start | bytes 580616 | tf_op jit(solution)/shard_map/ppermute | solution.py:30
  53.6 9.0 %collective-permute-start.21 = (f32[56,864]{1,0:T(8,128)S(1)}, f32[56,864]{1,0:T(8,128)S(1)}, u32[]{:S(2)}, u32[]{:S(2)}) collective-permute-start(f32[56,864]{1,0:T(8,128)S(1)} %get-tuple-element.74), channel_id=1, source_target_pairs={{0,56},{8,0},{16,8},{24,16},{32,24},{40,32},{48,40},{56,48},{1,57}... | collective-permute-start | bytes 580616 | tf_op jit(solution)/shard_map/ppermute | solution.py:30
  53.6 13.3 %collective-permute-start.18 = (f32[56,864]{1,0:T(8,128)S(1)}, f32[56,864]{1,0:T(8,128)S(1)}, u32[]{:S(2)}, u32[]{:S(2)}) collective-permute-start(f32[56,864]{1,0:T(8,128)S(1)} %get-tuple-element.70), channel_id=1, source_target_pairs={{0,56},{8,0},{16,8},{24,16},{32,24},{40,32},{48,40},{56,48},{1,57}... | collective-permute-start | bytes 580616 | tf_op jit(solution)/shard_map/ppermute | solution.py:30
  53.6 13.4 %collective-permute-start.25 = (f32[56,864]{1,0:T(8,128)S(1)}, f32[56,864]{1,0:T(8,128)S(1)}, u32[]{:S(2)}, u32[]{:S(2)}) collective-permute-start(f32[56,864]{1,0:T(8,128)S(1)} %get-tuple-element.78), channel_id=1, source_target_pairs={{0,8},{8,16},{16,24},{24,32},{32,40},{40,48},{48,56},{56,0},{1,9},... | collective-permute-start | bytes 580616 | tf_op jit(solution)/shard_map/ppermute | solution.py:30
  58.7 11.9 %collective-permute-start.15 = (f32[56,864]{1,0:T(8,128)S(1)}, f32[56,864]{1,0:T(8,128)S(1)}, u32[]{:S(2)}, u32[]{:S(2)}) collective-permute-start(f32[56,864]{1,0:T(8,128)S(1)} %add_block.10), channel_id=1, source_target_pairs={{0,8},{8,16},{16,24},{24,32},{32,40},{40,48},{48,56},{56,0},{1,9},... | collective-permute-start | bytes 580616 | tf_op jit(solution)/shard_map/ppermute | solution.py:30
  62.6 8.8 %collective-permute-start.22 = (f32[56,864]{1,0:T(8,128)S(1)}, f32[56,864]{1,0:T(8,128)S(1)}, u32[]{:S(2)}, u32[]{:S(2)}) collective-permute-start(f32[56,864]{1,0:T(8,128)S(1)} %add_block.15), channel_id=1, source_target_pairs={{0,56},{8,0},{16,8},{24,16},{32,24},{40,32},{48,40},{56,48},{1,57}... | collective-permute-start | bytes 580616 | tf_op jit(solution)/shard_map/ppermute | solution.py:30
  66.9 9.1 %collective-permute-start.19 = (f32[56,864]{1,0:T(8,128)S(1)}, f32[56,864]{1,0:T(8,128)S(1)}, u32[]{:S(2)}, u32[]{:S(2)}) collective-permute-start(f32[56,864]{1,0:T(8,128)S(1)} %add_block.13), channel_id=1, source_target_pairs={{0,56},{8,0},{16,8},{24,16},{32,24},{40,32},{48,40},{56,48},{1,57}... | collective-permute-start | bytes 580616 | tf_op jit(solution)/shard_map/ppermute | solution.py:30
  67.0 9.1 %collective-permute-start.26 = (f32[56,864]{1,0:T(8,128)S(1)}, f32[56,864]{1,0:T(8,128)S(1)}, u32[]{:S(2)}, u32[]{:S(2)}) collective-permute-start(f32[56,864]{1,0:T(8,128)S(1)} %add_block.18), channel_id=1, source_target_pairs={{0,8},{8,16},{16,24},{24,32},{32,40},{40,48},{48,56},{56,0},{1,9},... | collective-permute-start | bytes 580616 | tf_op jit(solution)/shard_map/ppermute | solution.py:30
  70.6 8.9 %collective-permute-start.16 = (f32[56,864]{1,0:T(8,128)S(1)}, f32[56,864]{1,0:T(8,128)S(1)}, u32[]{:S(2)}, u32[]{:S(2)}) collective-permute-start(f32[56,864]{1,0:T(8,128)S(1)} %add_block.11), channel_id=1, source_target_pairs={{0,8},{8,16},{16,24},{24,32},{32,40},{40,48},{48,56},{56,0},{1,9},... | collective-permute-start | bytes 580616 | tf_op jit(solution)/shard_map/ppermute | solution.py:30
  71.5 10.2 %collective-permute-start.23 = (f32[56,864]{1,0:T(8,128)S(1)}, f32[56,864]{1,0:T(8,128)S(1)}, u32[]{:S(2)}, u32[]{:S(2)}) collective-permute-start(f32[56,864]{1,0:T(8,128)S(1)} %add_block.16), channel_id=1, source_target_pairs={{0,56},{8,0},{16,8},{24,16},{32,24},{40,32},{48,40},{56,48},{1,57}... | collective-permute-start | bytes 580616 | tf_op jit(solution)/shard_map/ppermute | solution.py:30
  76.1 8.0 %collective-permute-start.20 = (f32[56,864]{1,0:T(8,128)S(1)}, f32[56,864]{1,0:T(8,128)S(1)}, u32[]{:S(2)}, u32[]{:S(2)}) collective-permute-start(f32[56,864]{1,0:T(8,128)S(1)} %add_block.14), channel_id=1, source_target_pairs={{0,56},{8,0},{16,8},{24,16},{32,24},{40,32},{48,40},{56,48},{1,57}... | collective-permute-start | bytes 580616 | tf_op jit(solution)/shard_map/ppermute | solution.py:30
  76.2 7.9 %collective-permute-start.27 = (f32[56,864]{1,0:T(8,128)S(1)}, f32[56,864]{1,0:T(8,128)S(1)}, u32[]{:S(2)}, u32[]{:S(2)}) collective-permute-start(f32[56,864]{1,0:T(8,128)S(1)} %add_block.19), channel_id=1, source_target_pairs={{0,8},{8,16},{16,24},{24,32},{32,40},{40,48},{48,56},{56,0},{1,9},... | collective-permute-start | bytes 580616 | tf_op jit(solution)/shard_map/ppermute | solution.py:30
  79.5 5.8 %collective-permute-start.17 = (f32[56,864]{1,0:T(8,128)S(1)}, f32[56,864]{1,0:T(8,128)S(1)}, u32[]{:S(2)}, u32[]{:S(2)}) collective-permute-start(f32[56,864]{1,0:T(8,128)S(1)} %add_block.12), channel_id=1, source_target_pairs={{0,8},{8,16},{16,24},{24,32},{32,40},{40,48},{48,56},{56,0},{1,9},... | collective-permute-start | bytes 580616 | tf_op jit(solution)/shard_map/ppermute | solution.py:30
  81.7 7.0 %collective-permute-start.24 = (f32[56,864]{1,0:T(8,128)S(1)}, f32[56,864]{1,0:T(8,128)S(1)}, u32[]{:S(2)}, u32[]{:S(2)}) collective-permute-start(f32[56,864]{1,0:T(8,128)S(1)} %add_block.17), channel_id=1, source_target_pairs={{0,56},{8,0},{16,8},{24,16},{32,24},{40,32},{48,40},{56,48},{1,57}... | collective-permute-start | bytes 580616 | tf_op jit(solution)/shard_map/ppermute | solution.py:30

commit v3 on v2

--- a/solution.py
+++ b/solution.py
@@ -12,6 +12,7 @@
 GELU_C = 0.7978845608028654
 NY, NZ, NX, NC = 4, 8, 4, 2
 OWN_MIB = 48
+PREP_MIB = 56
 F32 = jnp.float32
 BF16 = jnp.bfloat16
 
@@ -49,40 +50,38 @@
     return dot(matrix, matrix, ((1,), (1,)))
 
 
-def prepare_kernel(x_ref, dy_ref, out_ref, token_ref):
-    token_ref[...] = jnp.zeros(token_ref.shape, F32)
+def prepare_kernel(x_ref, dy_ref, mine_ref, x_out, dy_out):
+    x_out[...] = x_ref[...]
+    dy_out[...] = dy_ref[...]
     first = lax.axis_index("core") == 0
 
     @pl.when(first)
     def _():
-        out_ref[...] = x_ref[...].astype(F32)
+        mine_ref[...] = x_ref[...].astype(F32)
 
     @pl.when(jnp.logical_not(first))
     def _():
-        out_ref[...] = dy_ref[...].astype(F32)
+        mine_ref[...] = dy_ref[...].astype(F32)
 
 
 def own_kernel(
-    x_hbm, dy_hbm, wg_hbm, wu_hbm, wd_hbm, token_ref, g_ref, u_ref, h_ref, keep_ref, give_ref, wg, wu, wd,
-    x_ref, dy_ref, rows_ref, sems,
+    x_ref, dy_ref, wg_hbm, wu_hbm, wd_hbm, g_ref, u_ref, h_ref, keep_ref, give_ref, wg, wu, wd, rows_ref, sems
 ):
-    pairs = ((x_hbm, x_ref), (wg_hbm, wg), (wu_hbm, wu), (dy_hbm, dy_ref), (wd_hbm, wd))
+    pairs = ((wg_hbm, wg), (wu_hbm, wu), (wd_hbm, wd))
     copies = [pltpu.make_async_copy(a, b, sems.at[i]) for i, (a, b) in enumerate(pairs)]
     for copy in copies:
         copy.start()
+    x = x_ref[...]
+    dy = dy_ref[...]
+    gram_x = gram(x)
+    gram_dy = gram(dy)
     copies[0].wait()
-    x = x_ref[...]
-    gram_x = gram(x)
-    copies[1].wait()
     gate_pre = dot(x, wg[...], ((1,), (1,)))
     activated, gelu_slope = gelu_parts(gate_pre)
-    copies[2].wait()
+    copies[1].wait()
     up_pre = dot(x, wu[...], ((1,), (1,)))
     h = (activated * up_pre).astype(BF16)
-    copies[3].wait()
-    dy = dy_ref[...]
-    gram_dy = gram(dy)
-    copies[4].wait()
+    copies[2].wait()
     hidden_grad = dot(dy, wd[...], ((1,), (1,)))
     g = (hidden_grad * up_pre * gelu_slope).astype(BF16)
     u = (hidden_grad * activated).astype(BF16)
@@ -117,20 +116,27 @@
     scale_ref[...] = jnp.minimum(1.0, CLIP_NORM / jnp.sqrt(later_ref[0] + own)) * factor
 
 
-def order_kernel(array_ref, token_ref, out_ref):
+def forward_kernel(up_ref, down_ref, token_ref, up_out, down_out, low_ref, high_ref):
+    half = low_ref.shape[0]
+    low_ref[...] = up_ref[:half]
+    high_ref[...] = down_ref[half:]
+
+
+def order_kernel(*refs):
     pass
 
 
-def after(array, token):
+def after(token, *arrays):
+    hbm = pl.BlockSpec(memory_space=pl.ANY)
     return pl.pallas_call(
         order_kernel,
-        out_shape=jax.ShapeDtypeStruct(array.shape, array.dtype),
-        in_specs=[pl.BlockSpec(memory_space=pl.ANY)] * 2,
-        out_specs=pl.BlockSpec(memory_space=pl.ANY),
-        input_output_aliases={0: 0},
+        out_shape=[jax.ShapeDtypeStruct(a.shape, a.dtype) for a in arrays],
+        in_specs=[hbm] * (len(arrays) + 1),
+        out_specs=[hbm] * len(arrays),
+        input_output_aliases={i: i for i in range(len(arrays))},
         compiler_params=pltpu.CompilerParams(vmem_limit_bytes=1024 * 1024),
         name="order",
-    )(array, token)
+    )(*arrays, token)
 
 
 def merge(got_refs, swap_refs, xs, dys):
@@ -162,10 +168,10 @@
             target_ref[offset : offset + tokens, :] = source_ref[:, k * part : (k + 1) * part]
 
 
-def pair_kernel(
-    got0, got1, swap0, swap1, wg_ref, wu_ref, wd_ref, g_ref, u_ref, h_ref, xp_ref, dyp_ref, xs, dys
-):
-    merge((got0, got1), (swap0, swap1), xs, dys)
+def pair_kernel(*refs):
+    got, swap = refs[:2], refs[2:4]
+    wg_ref, wu_ref, wd_ref, g_ref, u_ref, h_ref, xp_ref, dyp_ref, xs, dys = refs[4:]
+    merge(got, swap, xs, dys)
     take_part(xs, xp_ref, 0)
     take_part(dys, dyp_ref, 0)
     g, u, h = forward(xs[...], dys[...], wg_ref[...], wu_ref[...], wd_ref[...])
@@ -176,13 +182,13 @@
 
 def last_kernel(
     scale0, scale1, scale2, scale3, x_ref, dy_ref, g_ref, u_ref, h_ref, g12_ref, u12_ref, h12_ref, xp_ref, dyp_ref,
-    got, swap, wg_ref, wu_ref, wd_ref, *refs,
+    got0, got1, swap0, swap1, wg_ref, wu_ref, wd_ref, *refs,
 ):
     out_refs = refs[: 2 * NZ]
     xs, dys, x_part, dy_part, blocks = refs[2 * NZ :]
     tokens, width = x_ref.shape
     part = width // NY
-    merge((got,), (swap,), xs, dys)
+    merge((got0, got1), (swap0, swap1), xs, dys)
     take_part(x_ref, x_part, 0)
     take_part(dy_ref, dy_part, 0)
     take_part(xs, x_part, 3 * tokens)
@@ -265,19 +271,18 @@
             name=name,
         )(*args)
 
-    mine, token = call(
-        prepare_kernel, "prepare", [shape(tokens, width), shape(8, 128)], [], 0, 4, inputs, out_grad
-    )
-    got = [shift(mine, "y", k) for k in (1, 3, 2)]
+    inside = shape(tokens, width, dtype=BF16)
+    mine, inputs, out_grad = call(
+        prepare_kernel, "prepare", [shape(tokens, width), inside, inside], [], 0, PREP_MIB, inputs, out_grad
+    )
+    up, down = shift(mine, "y", 1), shift(mine, "y", -1)
 
     hiddens = [shape(tokens, ff, dtype=BF16)] * 3
     group = shape(NX + 1, slice_rows, width)
     *own_back, keep, give, wg, wu, wd = call(
         own_kernel, "own_example", hiddens + [group] * 2 + [shape(ff, width, dtype=BF16)] * 3,
-        [pltpu.VMEM((tokens, width), BF16)] * 2
-        + [pltpu.VMEM((NX * NC, slice_rows, width), F32), pltpu.SemaphoreType.DMA((5,))],
-        0, OWN_MIB, inputs, out_grad, *weights, shift(token, "core", 1),
-        spaces=[(i, pl.ANY) for i in range(6)],
+        [pltpu.VMEM((NX * NC, slice_rows, width), F32), pltpu.SemaphoreType.DMA((3,))],
+        0, OWN_MIB, inputs, out_grad, *weights, spaces=[(i, pl.ANY) for i in (2, 3, 4)],
     )
     weights = (wg, wu, wd)
     one = shape(slice_rows + 8, width)
@@ -294,18 +299,32 @@
     )
     scales = [scale] + [shift(scale, "y", k) for k in (1, 3, 2)]
 
-    got = [after(a, t) for a, t in zip(got, (rest[2], rest[2], scale))]
-    swapped = [shift(a, "core", 1) for a in got]
+    half = shape(tokens // 2, width)
+    any_space = pl.BlockSpec(memory_space=pl.ANY)
+    vmem_space = pl.BlockSpec(memory_space=pltpu.VMEM)
+    up, down, low, high = pl.pallas_call(
+        forward_kernel,
+        out_shape=[shape(tokens, width), shape(tokens, width), half, half],
+        in_specs=[vmem_space, vmem_space, any_space],
+        out_specs=[vmem_space, vmem_space, vmem_space, vmem_space],
+        input_output_aliases={0: 0, 1: 1},
+        compiler_params=pltpu.CompilerParams(vmem_limit_bytes=8 * 1024 * 1024),
+        name="forward",
+    )(up, down, give)
+    far = [shift(low, "y", 1), shift(high, "y", -1)]
+    near = after(rest[2], up, down)
+    near_swap = [shift(a, "core", 1) for a in near]
+    far_swap = [shift(a, "core", 1) for a in far]
     both = [shape(2 * tokens, ff, dtype=BF16)] * 3 + [shape(2 * tokens, part, dtype=BF16)] * 2
     pair_back = call(
         pair_kernel, "pair_examples", both, [pltpu.VMEM((2 * tokens, width), BF16)] * 2, 6, 16,
-        *got[:2], *swapped[:2], *weights,
+        *near, *near_swap, *weights,
     )
     blocks = call(
         last_kernel, "group_gradients", [shape(half_rows, ff)] * (2 * NZ),
         [pltpu.VMEM((tokens, width), BF16)] * 2 + [pltpu.VMEM((NY * tokens, part), BF16)] * 2
         + [pltpu.VMEM((NZ, 2, half_rows, ff), F32)], 6, 20,
-        *scales, inputs, out_grad, *own_back, *pair_back, got[2], swapped[2], *weights,
+        *scales, inputs, out_grad, *own_back, *pair_back, *far, *far_swap, *weights,
     )
     plan = ((0, 1, 4), (1, -1, 4), (1, 1, 3), (0, -1, 3))
     held = [blocks[2 * (d * n % NZ) + i] for i, d, n in plan]

time: 89.9 us -> 87.8 us (0.977)
  starting transfers between devices: 43.4 us -> 39.7 us
  waiting for transfers between devices: 26.3 us -> 28.4 us
  local copies, waits for them, and re-layouts: 3.84 us -> 1.93 us
  Pallas kernels: 14.5 us -> 16.1 us
    ppermute x28 -> x29, starting transfers between devices: 43.4 us -> 39.7 us  [shift(): lax.ppermute(array, axis, [(i, (i + step) % size) for i in range(size)])]
    ppermute x28 -> x29, waiting for transfers between devices: 26.3 us -> 28.4 us  [shift(): lax.ppermute(array, axis, [(i, (i + step) % size) for i in range(size)])]
    unnamed x10 -> x6, local copies, waits for them, and re-layouts: 3.84 us -> 1.93 us
    pallas_call x17, Pallas kernels: 14.5 us -> 16.1 us  [call(): pl.pallas_call(kernel, out_shape=outs, in_specs=[pl.BlockSpec(memory_spac...]
  transfers between devices with their start and end apart: 28 -> 29, of which waited for: 13 -> 12; matrix products, arithmetic and copies ran while one was open for 0% -> 0% of each run, Pallas kernels for 11% -> 11%
where the time goes in v3:
time: 87.8 us; the launch traced here: 87.6 us
  starting transfers between devices  39.7 us (45%)
  waiting for transfers between devices  28.4 us (32%)
  Pallas kernels  16.1 us (18%)
  local copies, waits for them, and re-layouts  1.93 us (2%)
  between operations  1.44 us (2%)
    ppermute x29, starting transfers between devices, shift(): lax.ppermute(array, axis, [(i, (i + step) % size) for i in range(size)])  39.7 us
    ppermute x29, waiting for transfers between devices, shift(): lax.ppermute(array, axis, [(i, (i + step) % size) for i in range(size)])  28.4 us
    pallas_call x17, Pallas kernels, call(): pl.pallas_call(kernel, out_shape=outs, in_specs=[pl.BlockSpec(memory_spac...  16.1 us
    unnamed x6, local copies, waits for them, and re-layouts  1.93 us
  transfers between devices with their start and end apart: 29, of which 12 were waited for; matrix products, arithmetic and copies ran while one was open for 0% of the time, Pallas kernels for 11%

profile of v3, /device:TPU:96, one launch (start us, length us, event | category | flops | bytes accessed | tf_op | source)
XLA Modules:
  0.0 87.6 jit_solution(7770626002599312963)
XLA Ops:
  0.6 2.2 %prepare.1 = (f32[128,1152]{1,0:T(8,128)}, bf16[128,1152]{1,0:T(8,128)(2,1)}, bf16[128,1152]{1,0:T(8,128)(2,1)}) custom-call(bf16[128,1152]{1,0:T(8,128)(2,1)} %x_ref.1, bf16[128,1152]{1,0:T(8,128)(2,1)} %dy_ref.1), custom_call_target="tpu_custom_call" | custom-call | tf_op jit(solution)/shard_map/prepare/pallas_call | solution.py:259
  2.8 3.0 %collective-permute-start.8 = (f32[128,1152]{1,0:T(8,128)}, f32[128,1152]{1,0:T(8,128)S(1)}, u32[]{:S(2)}, u32[]{:S(2)}) collective-permute-start(f32[128,1152]{1,0:T(8,128)} %get-tuple-element.64), channel_id=1, source_target_pairs={{0,192},{64,0},{128,64},{192,128},{1,193},{65,1},{129,65},{193,129... | collective-permute-start | bytes 1769480 | tf_op jit(solution)/shard_map/ppermute | solution.py:31
  5.8 0.0 collective-permute-start.7
  5.8 1.0 %copy-done = bf16[128,1152]{1,0:T(8,128)(2,1)S(1)} copy-done((bf16[128,1152]{1,0:T(8,128)(2,1)S(1)}, bf16[128,1152]{1,0:T(8,128)(2,1)}, u32[]{:S(2)}) %copy-start) | copy-done | bytes 294936
  6.8 1.0 %copy-done.1 = bf16[128,1152]{1,0:T(8,128)(2,1)S(1)} copy-done((bf16[128,1152]{1,0:T(8,128)(2,1)S(1)}, bf16[128,1152]{1,0:T(8,128)(2,1)}, u32[]{:S(2)}) %copy-start.1) | copy-done | bytes 294936
  7.7 6.1 %own_example.1 = (bf16[128,864]{1,0:T(8,128)(2,1)S(1)}, bf16[128,864]{1,0:T(8,128)(2,1)S(1)}, bf16[128,864]{1,0:T(8,128)(2,1)S(1)}, f32[5,16,1152]{2,1,0:T(8,128...) custom-call(bf16[128,1152]{1,0:T(8,128)(2,1)S(1)} %copy-done, ...), custom_call_target="tpu_custom_call" | custom-call | tf_op jit(solution)/shard_map/own_example/pallas_call | solution.py:259
  13.9 0.1 collective-permute-start
  14.0 1.7 %collective-permute-done.got_ref = f32[5,16,1152]{2,1,0:T(8,128)S(1)} collective-permute-done((f32[5,16,1152]{2,1,0:T(8,128)S(1)}, f32[5,16,1152]{2,1,0:T(8,128)S(1)}, u32[]{:S(2)}, u32[]{:S(2)}) %collective-permute-start) | collective-permute-done | bytes 368672 | tf_op jit(solution)/shard_map/ppermute | solution.py:31
  15.6 0.1 input_spread.1
  15.7 3.1 %collective-permute-start.3 = (f32[24,1152]{1,0:T(8,128)S(1)}, f32[24,1152]{1,0:T(8,128)S(1)}, u32[]{:S(2)}, u32[]{:S(2)}) collective-permute-start(f32[24,1152]{1,0:T(8,128)S(1)} %get-tuple-element.58), channel_id=1, source_target_pairs={{0,4},{2,6},{4,0},{6,2},{1,5},{3,7},{5,1},{7,3},{8,12},{10,14},{12... | collective-permute-start | bytes 331784 | tf_op jit(solution)/shard_map/ppermute | solution.py:31
  18.8 0.0 collective-permute-done.8.down_ref
  18.8 3.2 %collective-permute-done.7.up_ref = f32[128,1152]{1,0:T(8,128)S(1)} collective-permute-done((f32[128,1152]{1,0:T(8,128)}, f32[128,1152]{1,0:T(8,128)S(1)}, u32[]{:S(2)}, u32[]{:S(2)}) %collective-permute-start.7) | collective-permute-done | bytes 589856 | tf_op jit(solution)/shard_map/ppermute | solution.py:31
  22.1 0.3 collective-permute-done.3.got2.refs_2_
  22.4 0.0 collective-permute-start.9
  22.4 0.5 collective-permute-start.10
  22.9 0.6 collective-permute-start.11
  23.5 2.7 %collective-permute-start.12 = (f32[64,1152]{1,0:T(8,128)S(1)}, f32[64,1152]{1,0:T(8,128)S(1)}, u32[]{:S(2)}, u32[]{:S(2)}) collective-permute-start(f32[64,1152]{1,0:T(8,128)S(1)} %get-tuple-element.78), channel_id=1, source_target_pairs={{0,192},{64,0},{128,64},{192,128},{1,193},{65,1},{129,65},{193,129... | collective-permute-start | bytes 884744 | tf_op jit(solution)/shard_map/ppermute | solution.py:31
  26.1 1.5 %collective-permute-start.1 = (f32[24,1152]{1,0:T(8,128)S(1)}, f32[24,1152]{1,0:T(8,128)S(1)}, u32[]{:S(2)}, u32[]{:S(2)}) collective-permute-start(f32[24,1152]{1,0:T(8,128)S(1)} %get-tuple-element.56), channel_id=1, source_target_pairs={{0,2},{2,4},{4,6},{6,0},{1,3},{3,5},{5,7},{7,1},{8,10},{10,12},{12... | collective-permute-start | bytes 331784 | tf_op jit(solution)/shard_map/ppermute | solution.py:31
  27.6 4.5 %collective-permute-done.1.got1 = f32[24,1152]{1,0:T(8,128)S(1)} collective-permute-done((f32[24,1152]{1,0:T(8,128)S(1)}, f32[24,1152]{1,0:T(8,128)S(1)}, u32[]{:S(2)}, u32[]{:S(2)}) %collective-permute-start.1) | collective-permute-done | bytes 110624 | tf_op jit(solution)/shard_map/ppermute | solution.py:31
  32.1 1.5 %collective-permute-start.2 = (f32[24,1152]{1,0:T(8,128)S(1)}, f32[24,1152]{1,0:T(8,128)S(1)}, u32[]{:S(2)}, u32[]{:S(2)}) collective-permute-start(f32[24,1152]{1,0:T(8,128)S(1)} %get-tuple-element.57), channel_id=1, source_target_pairs={{0,6},{2,0},{4,2},{6,4},{1,7},{3,1},{5,3},{7,5},{8,14},{10,8},{12,... | collective-permute-start | bytes 331784 | tf_op jit(solution)/shard_map/ppermute | solution.py:31
  33.6 0.0 collective-permute-done.11.got0
  33.6 0.0 collective-permute-start.13
  33.6 0.0 collective-permute-done.12.got1
  33.7 0.5 collective-permute-start.14
  34.8 2.0 %collective-permute-done.2.got3 = f32[24,1152]{1,0:T(8,128)S(1)} collective-permute-done((f32[24,1152]{1,0:T(8,128)S(1)}, f32[24,1152]{1,0:T(8,128)S(1)}, u32[]{:S(2)}, u32[]{:S(2)}) %collective-permute-start.2) | collective-permute-done | bytes 110624 | tf_op jit(solution)/shard_map/ppermute | solution.py:31
  36.8 0.6 input_sum.1
  37.5 1.5 %collective-permute-start.6 = (f32[8,128]{1,0:T(8,128)S(1)}, f32[8,128]{1,0:T(8,128)S(1)}, u32[]{:S(2)}, u32[]{:S(2)}) collective-permute-start(f32[8,128]{1,0:T(8,128)S(1)} %get-tuple-element.60.scale0), channel_id=1, source_target_pairs={{0,128},{64,192},{128,0},{192,64},{1,129},{65,193},{129,1},{193,65... | collective-permute-start | bytes 12296 | tf_op jit(solution)/shard_map/ppermute | solution.py:31
  38.9 0.0 collective-permute-done.9.refs_2_
  39.0 0.6 collective-permute-start.5
  39.5 0.0 collective-permute-done.10.refs_3_
  39.5 1.4 %collective-permute-start.4 = (f32[8,128]{1,0:T(8,128)S(1)}, f32[8,128]{1,0:T(8,128)S(1)}, u32[]{:S(2)}, u32[]{:S(2)}) collective-permute-start(f32[8,128]{1,0:T(8,128)S(1)} %get-tuple-element.60.scale0), channel_id=1, source_target_pairs={{0,64},{64,128},{128,192},{192,0},{1,65},{65,129},{129,193},{193,1... | collective-permute-start | bytes 12296 | tf_op jit(solution)/shard_map/ppermute | solution.py:31
  41.0 2.6 %pair_examples.1 = (bf16[256,864]{1,0:T(8,128)(2,1)S(1)}, bf16[256,864]{1,0:T(8,128)(2,1)S(1)}, bf16[256,864]{1,0:T(8,128)(2,1)S(1)}, bf16[256,288]{1,0:T(8,128)(2,1)S(1)}, bf16[256,288]{1,0:T(8,128)(2,1)S(1)}) custom-call(f32[128,1152]{1,0:T(8,128)S(1)} %get-tuple-element.67.refs_0_, f32[128,1152]{1,0:T(8,128)S(1)} %get-tuple-element.68.refs_1_, ...), custom_call_target="tpu_custom_call" | custom-call | flops 3057647616 | bytes 8331264 | tf_op jit(solution)/shard_map/pair_examples/pallas_call | solution.py:259
  43.6 0.0 collective-permute-done.6.scale3
  43.6 0.0 collective-permute-done.5.scale2
  43.6 0.8 collective-permute-done.4.scale1
  44.4 0.0 collective-permute-done.13.swap0
  44.4 0.0 collective-permute-done.14.swap1
  44.4 3.4 %group_gradients.1 = (f32[56,864]{1,0:T(8,128)S(1)}, f32[56,864]{1,0:T(8,128)S(1)}, f32[56,864]{1,0:T(8,128)S(1)}, f32[56,864]{1,0:T(8,128)S(1)}, f32[56,864]{1,...) custom-call(f32[8,128]{1,0:T(8,128)S(1)} %get-tuple-element.60.scale, ...), custom_call_target="tpu_custom_call" | custom-call | flops 3057647616 | bytes 10043392 | tf_op jit(solution)/shard_map/group_gradients/pallas_call | solution.py:259
  47.8 3.2 %collective-permute-start.15 = (f32[56,864]{1,0:T(8,128)S(1)}, f32[56,864]{1,0:T(8,128)S(1)}, u32[]{:S(2)}, u32[]{:S(2)}) collective-permute-start(f32[56,864]{1,0:T(8,128)S(1)} %get-tuple-element.80), channel_id=1, source_target_pairs={{0,8},{8,16},{16,24},{24,32},{32,40},{40,48},{48,56},{56,0},{1,9},... | collective-permute-start | bytes 580616 | tf_op jit(solution)/shard_map/ppermute | solution.py:31
  51.0 0.0 collective-permute-start.22
  51.0 0.0 collective-permute-start.19
  51.0 3.3 %collective-permute-start.26 = (f32[56,864]{1,0:T(8,128)S(1)}, f32[56,864]{1,0:T(8,128)S(1)}, u32[]{:S(2)}, u32[]{:S(2)}) collective-permute-start(f32[56,864]{1,0:T(8,128)S(1)} %get-tuple-element.92), channel_id=1, source_target_pairs={{0,8},{8,16},{16,24},{24,32},{32,40},{40,48},{48,56},{56,0},{1,9},... | collective-permute-start | bytes 580616 | tf_op jit(solution)/shard_map/ppermute | solution.py:31
  54.3 2.1 %collective-permute-done.15.a_ref = f32[56,864]{1,0:T(8,128)S(1)} collective-permute-done((f32[56,864]{1,0:T(8,128)S(1)}, f32[56,864]{1,0:T(8,128)S(1)}, u32[]{:S(2)}, u32[]{:S(2)}) %collective-permute-start.15) | collective-permute-done | bytes 193568 | tf_op jit(solution)/shard_map/ppermute | solution.py:31
  56.4 3.8 %collective-permute-start.16 = (f32[56,864]{1,0:T(8,128)S(1)}, f32[56,864]{1,0:T(8,128)S(1)}, u32[]{:S(2)}, u32[]{:S(2)}) collective-permute-start(f32[56,864]{1,0:T(8,128)S(1)} %add_block.10), channel_id=1, source_target_pairs={{0,8},{8,16},{16,24},{24,32},{32,40},{40,48},{48,56},{56,0},{1,9},... | collective-permute-start | bytes 580616 | tf_op jit(solution)/shard_map/ppermute | solution.py:31
  60.2 0.0 collective-permute-done.22.a_ref
  60.2 0.1 collective-permute-start.23
  60.3 3.4 %collective-permute-done.19.a_ref = f32[56,864]{1,0:T(8,128)S(1)} collective-permute-done((f32[56,864]{1,0:T(8,128)S(1)}, f32[56,864]{1,0:T(8,128)S(1)}, u32[]{:S(2)}, u32[]{:S(2)}) %collective-permute-start.19) | collective-permute-done | bytes 193568 | tf_op jit(solution)/shard_map/ppermute | solution.py:31
  63.7 0.3 collective-permute-start.20
  64.0 0.0 collective-permute-done.26.a_ref
  64.0 3.3 %collective-permute-start.27 = (f32[56,864]{1,0:T(8,128)S(1)}, f32[56,864]{1,0:T(8,128)S(1)}, u32[]{:S(2)}, u32[]{:S(2)}) collective-permute-start(f32[56,864]{1,0:T(8,128)S(1)} %add_block.18), channel_id=1, source_target_pairs={{0,8},{8,16},{16,24},{24,32},{32,40},{40,48},{48,56},{56,0},{1,9},... | collective-permute-start | bytes 580616 | tf_op jit(solution)/shard_map/ppermute | solution.py:31
  67.4 1.9 %collective-permute-start.17 = (f32[56,864]{1,0:T(8,128)S(1)}, f32[56,864]{1,0:T(8,128)S(1)}, u32[]{:S(2)}, u32[]{:S(2)}) collective-permute-start(f32[56,864]{1,0:T(8,128)S(1)} %add_block.11), channel_id=1, source_target_pairs={{0,8},{8,16},{16,24},{24,32},{32,40},{40,48},{48,56},{56,0},{1,9},... | collective-permute-start | bytes 580616 | tf_op jit(solution)/shard_map/ppermute | solution.py:31
  69.2 0.3 collective-permute-start.24
  69.6 3.5 %collective-permute-done.20.a_ref = f32[56,864]{1,0:T(8,128)S(1)} collective-permute-done((f32[56,864]{1,0:T(8,128)S(1)}, f32[56,864]{1,0:T(8,128)S(1)}, u32[]{:S(2)}, u32[]{:S(2)}) %collective-permute-start.20) | collective-permute-done | bytes 193568 | tf_op jit(solution)/shard_map/ppermute | solution.py:31
  73.1 0.1 collective-permute-start.21
  73.2 0.0 collective-permute-done.27.a_ref
  73.2 3.3 %collective-permute-start.28 = (f32[56,864]{1,0:T(8,128)S(1)}, f32[56,864]{1,0:T(8,128)S(1)}, u32[]{:S(2)}, u32[]{:S(2)}) collective-permute-start(f32[56,864]{1,0:T(8,128)S(1)} %add_block.19), channel_id=1, source_target_pairs={{0,8},{8,16},{16,24},{24,32},{32,40},{40,48},{48,56},{56,0},{1,9},... | collective-permute-start | bytes 580616 | tf_op jit(solution)/shard_map/ppermute | solution.py:31
  76.5 3.2 %collective-permute-start.18 = (f32[56,864]{1,0:T(8,128)S(1)}, f32[56,864]{1,0:T(8,128)S(1)}, u32[]{:S(2)}, u32[]{:S(2)}) collective-permute-start(f32[56,864]{1,0:T(8,128)S(1)} %add_block.12), channel_id=1, source_target_pairs={{0,8},{8,16},{16,24},{24,32},{32,40},{40,48},{48,56},{56,0},{1,9},... | collective-permute-start | bytes 580616 | tf_op jit(solution)/shard_map/ppermute | solution.py:31
  79.8 0.0 collective-permute-done.24.a_ref
  79.8 0.1 collective-permute-start.25
  79.9 0.7 collective-permute-done.21.top2
  80.6 0.0 collective-permute-done.28.low2
  80.6 2.4 %collective-permute-done.18.top1 = f32[56,864]{1,0:T(8,128)S(1)} collective-permute-done((f32[56,864]{1,0:T(8,128)S(1)}, f32[56,864]{1,0:T(8,128)S(1)}, u32[]{:S(2)}, u32[]{:S(2)}) %collective-permute-start.18) | collective-permute-done | bytes 193568 | tf_op jit(solution)/shard_map/ppermute | solution.py:31
  83.0 3.8 %collective-permute-done.25.low1 = f32[56,864]{1,0:T(8,128)S(1)} collective-permute-done((f32[56,864]{1,0:T(8,128)S(1)}, f32[56,864]{1,0:T(8,128)S(1)}, u32[]{:S(2)}, u32[]{:S(2)}) %collective-permute-start.25) | collective-permute-done | bytes 193568 | tf_op jit(solution)/shard_map/ppermute | solution.py:31
  86.8 0.8 finish.1
  (19 shorter events, 0.3 us)
Async XLA Ops:
  2.8 16.0 %collective-permute-start.8 = (f32[128,1152]{1,0:T(8,128)}, f32[128,1152]{1,0:T(8,128)S(1)}, u32[]{:S(2)}, u32[]{:S(2)}) collective-permute-start(f32[128,1152]{1,0:T(8,128)} %get-tuple-element.64), channel_id=1, source_target_pairs={{0,192},{64,0},{128,64},{192,128},{1,193},{65,1},{129,65},{193,129... | collective-permute-start | bytes 1769480 | tf_op jit(solution)/shard_map/ppermute | solution.py:31
  5.8 16.2 %collective-permute-start.7 = (f32[128,1152]{1,0:T(8,128)}, f32[128,1152]{1,0:T(8,128)S(1)}, u32[]{:S(2)}, u32[]{:S(2)}) collective-permute-start(f32[128,1152]{1,0:T(8,128)} %get-tuple-element.64), channel_id=1, source_target_pairs={{0,64},{64,128},{128,192},{192,0},{1,65},{65,129},{129,193},{193,1... | collective-permute-start | bytes 1769480 | tf_op jit(solution)/shard_map/ppermute | solution.py:31
  5.8 1.0 %copy-start = (bf16[128,1152]{1,0:T(8,128)(2,1)S(1)}, bf16[128,1152]{1,0:T(8,128)(2,1)}, u32[]{:S(2)}) copy-start(bf16[128,1152]{1,0:T(8,128)(2,1)} %get-tuple-element.51.x_ref) | copy-start | bytes 884740
  6.8 1.0 %copy-start.1 = (bf16[128,1152]{1,0:T(8,128)(2,1)S(1)}, bf16[128,1152]{1,0:T(8,128)(2,1)}, u32[]{:S(2)}) copy-start(bf16[128,1152]{1,0:T(8,128)(2,1)} %get-tuple-element.52.dy_ref) | copy-start | bytes 884740
  13.9 1.8 %collective-permute-start = (f32[5,16,1152]{2,1,0:T(8,128)S(1)}, f32[5,16,1152]{2,1,0:T(8,128)S(1)}, u32[]{:S(2)}, u32[]{:S(2)}) collective-permute-start(f32[5,16,1152]{2,1,0:T(8,128)S(1)} %get-tuple-element.54.token_ref), channel_id=1, source_target_pairs={{0,1},{1,0},{2,3},{3,2},{4,5},{5,4},{6,7},{7,6},{8,9},{9,8},{10,11... | collective-permute-start | bytes 1105928 | tf_op jit(solution)/shard_map/ppermute | solution.py:31
  15.6 25.4 %copy-start.2 = (bf16[864,1152]{1,0:T(8,128)(2,1)S(1)}, bf16[864,1152]{1,0:T(8,128)(2,1)}, u32[]{:S(2)}) copy-start(bf16[864,1152]{1,0:T(8,128)(2,1)} %get-tuple-element.71.refs_6_.wd_ref) | copy-start | bytes 5971972
  15.7 6.7 %collective-permute-start.3 = (f32[24,1152]{1,0:T(8,128)S(1)}, f32[24,1152]{1,0:T(8,128)S(1)}, u32[]{:S(2)}, u32[]{:S(2)}) collective-permute-start(f32[24,1152]{1,0:T(8,128)S(1)} %get-tuple-element.58), channel_id=1, source_target_pairs={{0,4},{2,6},{4,0},{6,2},{1,5},{3,7},{5,1},{7,3},{8,12},{10,14},{12... | collective-permute-start | bytes 331784 | tf_op jit(solution)/shard_map/ppermute | solution.py:31
  22.4 16.6 %collective-permute-start.9 = (f32[128,1152]{1,0:T(8,128)S(1)}, f32[128,1152]{1,0:T(8,128)S(1)}, u32[]{:S(2)}, u32[]{:S(2)}) collective-permute-start(f32[128,1152]{1,0:T(8,128)S(1)} %get-tuple-element.67.refs_0_), channel_id=1, source_target_pairs={{0,1},{1,0},{2,3},{3,2},{4,5},{5,4},{6,7},{7,6},{8,9},{9,8},{10,11... | collective-permute-start | bytes 1769480 | tf_op jit(solution)/shard_map/ppermute | solution.py:31
  22.4 17.1 %collective-permute-start.10 = (f32[128,1152]{1,0:T(8,128)S(1)}, f32[128,1152]{1,0:T(8,128)S(1)}, u32[]{:S(2)}, u32[]{:S(2)}) collective-permute-start(f32[128,1152]{1,0:T(8,128)S(1)} %get-tuple-element.68.refs_1_), channel_id=1, source_target_pairs={{0,1},{1,0},{2,3},{3,2},{4,5},{5,4},{6,7},{7,6},{8,9},{9,8},{10,11... | collective-permute-start | bytes 1769480 | tf_op jit(solution)/shard_map/ppermute | solution.py:31
  22.9 10.7 %collective-permute-start.11 = (f32[64,1152]{1,0:T(8,128)S(1)}, f32[64,1152]{1,0:T(8,128)S(1)}, u32[]{:S(2)}, u32[]{:S(2)}) collective-permute-start(f32[64,1152]{1,0:T(8,128)S(1)} %get-tuple-element.77), channel_id=1, source_target_pairs={{0,64},{64,128},{128,192},{192,0},{1,65},{65,129},{129,193},{193,1... | collective-permute-start | bytes 884744 | tf_op jit(solution)/shard_map/ppermute | solution.py:31
  23.5 10.2 %collective-permute-start.12 = (f32[64,1152]{1,0:T(8,128)S(1)}, f32[64,1152]{1,0:T(8,128)S(1)}, u32[]{:S(2)}, u32[]{:S(2)}) collective-permute-start(f32[64,1152]{1,0:T(8,128)S(1)} %get-tuple-element.78), channel_id=1, source_target_pairs={{0,192},{64,0},{128,64},{192,128},{1,193},{65,1},{129,65},{193,129... | collective-permute-start | bytes 884744 | tf_op jit(solution)/shard_map/ppermute | solution.py:31
  26.1 6.0 %collective-permute-start.1 = (f32[24,1152]{1,0:T(8,128)S(1)}, f32[24,1152]{1,0:T(8,128)S(1)}, u32[]{:S(2)}, u32[]{:S(2)}) collective-permute-start(f32[24,1152]{1,0:T(8,128)S(1)} %get-tuple-element.56), channel_id=1, source_target_pairs={{0,2},{2,4},{4,6},{6,0},{1,3},{3,5},{5,7},{7,1},{8,10},{10,12},{12... | collective-permute-start | bytes 331784 | tf_op jit(solution)/shard_map/ppermute | solution.py:31
  32.1 4.7 %collective-permute-start.2 = (f32[24,1152]{1,0:T(8,128)S(1)}, f32[24,1152]{1,0:T(8,128)S(1)}, u32[]{:S(2)}, u32[]{:S(2)}) collective-permute-start(f32[24,1152]{1,0:T(8,128)S(1)} %get-tuple-element.57), channel_id=1, source_target_pairs={{0,6},{2,0},{4,2},{6,4},{1,7},{3,1},{5,3},{7,5},{8,14},{10,8},{12,... | collective-permute-start | bytes 331784 | tf_op jit(solution)/shard_map/ppermute | solution.py:31
  33.6 10.7 %collective-permute-start.13 = (f32[64,1152]{1,0:T(8,128)S(1)}, f32[64,1152]{1,0:T(8,128)S(1)}, u32[]{:S(2)}, u32[]{:S(2)}) collective-permute-start(f32[64,1152]{1,0:T(8,128)S(1)} %collective-permute-done.11.got0), channel_id=1, source_target_pairs={{0,1},{1,0},{2,3},{3,2},{4,5},{5,4},{6,7},{7,6},{8,9},{9,8},{10,11... | collective-permute-start | bytes 884744 | tf_op jit(solution)/shard_map/ppermute | solution.py:31
  33.7 10.7 %collective-permute-start.14 = (f32[64,1152]{1,0:T(8,128)S(1)}, f32[64,1152]{1,0:T(8,128)S(1)}, u32[]{:S(2)}, u32[]{:S(2)}) collective-permute-start(f32[64,1152]{1,0:T(8,128)S(1)} %collective-permute-done.12.got1), channel_id=1, source_target_pairs={{0,1},{1,0},{2,3},{3,2},{4,5},{5,4},{6,7},{7,6},{8,9},{9,8},{10,11... | collective-permute-start | bytes 884744 | tf_op jit(solution)/shard_map/ppermute | solution.py:31
  37.5 6.1 %collective-permute-start.6 = (f32[8,128]{1,0:T(8,128)S(1)}, f32[8,128]{1,0:T(8,128)S(1)}, u32[]{:S(2)}, u32[]{:S(2)}) collective-permute-start(f32[8,128]{1,0:T(8,128)S(1)} %get-tuple-element.60.scale0), channel_id=1, source_target_pairs={{0,128},{64,192},{128,0},{192,64},{1,129},{65,193},{129,1},{193,65... | collective-permute-start | bytes 12296 | tf_op jit(solution)/shard_map/ppermute | solution.py:31
  39.0 4.6 %collective-permute-start.5 = (f32[8,128]{1,0:T(8,128)S(1)}, f32[8,128]{1,0:T(8,128)S(1)}, u32[]{:S(2)}, u32[]{:S(2)}) collective-permute-start(f32[8,128]{1,0:T(8,128)S(1)} %get-tuple-element.60.scale0), channel_id=1, source_target_pairs={{0,192},{64,0},{128,64},{192,128},{1,193},{65,1},{129,65},{193,129... | collective-permute-start | bytes 12296 | tf_op jit(solution)/shard_map/ppermute | solution.py:31
  39.5 4.8 %collective-permute-start.4 = (f32[8,128]{1,0:T(8,128)S(1)}, f32[8,128]{1,0:T(8,128)S(1)}, u32[]{:S(2)}, u32[]{:S(2)}) collective-permute-start(f32[8,128]{1,0:T(8,128)S(1)} %get-tuple-element.60.scale0), channel_id=1, source_target_pairs={{0,64},{64,128},{128,192},{192,0},{1,65},{65,129},{129,193},{193,1... | collective-permute-start | bytes 12296 | tf_op jit(solution)/shard_map/ppermute | solution.py:31
  47.8 8.6 %collective-permute-start.15 = (f32[56,864]{1,0:T(8,128)S(1)}, f32[56,864]{1,0:T(8,128)S(1)}, u32[]{:S(2)}, u32[]{:S(2)}) collective-permute-start(f32[56,864]{1,0:T(8,128)S(1)} %get-tuple-element.80), channel_id=1, source_target_pairs={{0,8},{8,16},{16,24},{24,32},{32,40},{40,48},{48,56},{56,0},{1,9},... | collective-permute-start | bytes 580616 | tf_op jit(solution)/shard_map/ppermute | solution.py:31
  51.0 9.2 %collective-permute-start.22 = (f32[56,864]{1,0:T(8,128)S(1)}, f32[56,864]{1,0:T(8,128)S(1)}, u32[]{:S(2)}, u32[]{:S(2)}) collective-permute-start(f32[56,864]{1,0:T(8,128)S(1)} %get-tuple-element.88), channel_id=1, source_target_pairs={{0,56},{8,0},{16,8},{24,16},{32,24},{40,32},{48,40},{56,48},{1,57}... | collective-permute-start | bytes 580616 | tf_op jit(solution)/shard_map/ppermute | solution.py:31
  51.0 12.7 %collective-permute-start.19 = (f32[56,864]{1,0:T(8,128)S(1)}, f32[56,864]{1,0:T(8,128)S(1)}, u32[]{:S(2)}, u32[]{:S(2)}) collective-permute-start(f32[56,864]{1,0:T(8,128)S(1)} %get-tuple-element.84), channel_id=1, source_target_pairs={{0,56},{8,0},{16,8},{24,16},{32,24},{40,32},{48,40},{56,48},{1,57}... | collective-permute-start | bytes 580616 | tf_op jit(solution)/shard_map/ppermute | solution.py:31
  51.0 13.0 %collective-permute-start.26 = (f32[56,864]{1,0:T(8,128)S(1)}, f32[56,864]{1,0:T(8,128)S(1)}, u32[]{:S(2)}, u32[]{:S(2)}) collective-permute-start(f32[56,864]{1,0:T(8,128)S(1)} %get-tuple-element.92), channel_id=1, source_target_pairs={{0,8},{8,16},{16,24},{24,32},{32,40},{40,48},{48,56},{56,0},{1,9},... | collective-permute-start | bytes 580616 | tf_op jit(solution)/shard_map/ppermute | solution.py:31
  56.4 10.9 %collective-permute-start.16 = (f32[56,864]{1,0:T(8,128)S(1)}, f32[56,864]{1,0:T(8,128)S(1)}, u32[]{:S(2)}, u32[]{:S(2)}) collective-permute-start(f32[56,864]{1,0:T(8,128)S(1)} %add_block.10), channel_id=1, source_target_pairs={{0,8},{8,16},{16,24},{24,32},{32,40},{40,48},{48,56},{56,0},{1,9},... | collective-permute-start | bytes 580616 | tf_op jit(solution)/shard_map/ppermute | solution.py:31
  60.2 9.0 %collective-permute-start.23 = (f32[56,864]{1,0:T(8,128)S(1)}, f32[56,864]{1,0:T(8,128)S(1)}, u32[]{:S(2)}, u32[]{:S(2)}) collective-permute-start(f32[56,864]{1,0:T(8,128)S(1)} %add_block.15), channel_id=1, source_target_pairs={{0,56},{8,0},{16,8},{24,16},{32,24},{40,32},{48,40},{56,48},{1,57}... | collective-permute-start | bytes 580616 | tf_op jit(solution)/shard_map/ppermute | solution.py:31
  63.7 9.4 %collective-permute-start.20 = (f32[56,864]{1,0:T(8,128)S(1)}, f32[56,864]{1,0:T(8,128)S(1)}, u32[]{:S(2)}, u32[]{:S(2)}) collective-permute-start(f32[56,864]{1,0:T(8,128)S(1)} %add_block.13), channel_id=1, source_target_pairs={{0,56},{8,0},{16,8},{24,16},{32,24},{40,32},{48,40},{56,48},{1,57}... | collective-permute-start | bytes 580616 | tf_op jit(solution)/shard_map/ppermute | solution.py:31
  64.0 9.1 %collective-permute-start.27 = (f32[56,864]{1,0:T(8,128)S(1)}, f32[56,864]{1,0:T(8,128)S(1)}, u32[]{:S(2)}, u32[]{:S(2)}) collective-permute-start(f32[56,864]{1,0:T(8,128)S(1)} %add_block.18), channel_id=1, source_target_pairs={{0,8},{8,16},{16,24},{24,32},{32,40},{40,48},{48,56},{56,0},{1,9},... | collective-permute-start | bytes 580616 | tf_op jit(solution)/shard_map/ppermute | solution.py:31
  67.4 9.2 %collective-permute-start.17 = (f32[56,864]{1,0:T(8,128)S(1)}, f32[56,864]{1,0:T(8,128)S(1)}, u32[]{:S(2)}, u32[]{:S(2)}) collective-permute-start(f32[56,864]{1,0:T(8,128)S(1)} %add_block.11), channel_id=1, source_target_pairs={{0,8},{8,16},{16,24},{24,32},{32,40},{40,48},{48,56},{56,0},{1,9},... | collective-permute-start | bytes 580616 | tf_op jit(solution)/shard_map/ppermute | solution.py:31
  69.2 10.5 %collective-permute-start.24 = (f32[56,864]{1,0:T(8,128)S(1)}, f32[56,864]{1,0:T(8,128)S(1)}, u32[]{:S(2)}, u32[]{:S(2)}) collective-permute-start(f32[56,864]{1,0:T(8,128)S(1)} %add_block.16), channel_id=1, source_target_pairs={{0,56},{8,0},{16,8},{24,16},{32,24},{40,32},{48,40},{56,48},{1,57}... | collective-permute-start | bytes 580616 | tf_op jit(solution)/shard_map/ppermute | solution.py:31
  73.1 7.5 %collective-permute-start.21 = (f32[56,864]{1,0:T(8,128)S(1)}, f32[56,864]{1,0:T(8,128)S(1)}, u32[]{:S(2)}, u32[]{:S(2)}) collective-permute-start(f32[56,864]{1,0:T(8,128)S(1)} %add_block.14), channel_id=1, source_target_pairs={{0,56},{8,0},{16,8},{24,16},{32,24},{40,32},{48,40},{56,48},{1,57}... | collective-permute-start | bytes 580616 | tf_op jit(solution)/shard_map/ppermute | solution.py:31
  73.2 7.4 %collective-permute-start.28 = (f32[56,864]{1,0:T(8,128)S(1)}, f32[56,864]{1,0:T(8,128)S(1)}, u32[]{:S(2)}, u32[]{:S(2)}) collective-permute-start(f32[56,864]{1,0:T(8,128)S(1)} %add_block.19), channel_id=1, source_target_pairs={{0,8},{8,16},{16,24},{24,32},{32,40},{40,48},{48,56},{56,0},{1,9},... | collective-permute-start | bytes 580616 | tf_op jit(solution)/shard_map/ppermute | solution.py:31
  76.5 6.4 %collective-permute-start.18 = (f32[56,864]{1,0:T(8,128)S(1)}, f32[56,864]{1,0:T(8,128)S(1)}, u32[]{:S(2)}, u32[]{:S(2)}) collective-permute-start(f32[56,864]{1,0:T(8,128)S(1)} %add_block.12), channel_id=1, source_target_pairs={{0,8},{8,16},{16,24},{24,32},{32,40},{40,48},{48,56},{56,0},{1,9},... | collective-permute-start | bytes 580616 | tf_op jit(solution)/shard_map/ppermute | solution.py:31
  79.8 7.0 %collective-permute-start.25 = (f32[56,864]{1,0:T(8,128)S(1)}, f32[56,864]{1,0:T(8,128)S(1)}, u32[]{:S(2)}, u32[]{:S(2)}) collective-permute-start(f32[56,864]{1,0:T(8,128)S(1)} %add_block.17), channel_id=1, source_target_pairs={{0,56},{8,0},{16,8},{24,16},{32,24},{40,32},{48,40},{56,48},{1,57}... | collective-permute-start | bytes 580616 | tf_op jit(solution)/shard_map/ppermute | solution.py:31

commit v4 on v3

--- a/solution.py
+++ b/solution.py
@@ -12,7 +12,7 @@
 GELU_C = 0.7978845608028654
 NY, NZ, NX, NC = 4, 8, 4, 2
 OWN_MIB = 48
-PREP_MIB = 56
+PREP_MIB = 8
 F32 = jnp.float32
 BF16 = jnp.bfloat16
 
@@ -108,7 +108,7 @@
         out_ref[size:, :] = rows_ref[NX, :8, :]
 
 
-def gather_kernel(mine_ref, got1, got3, got2, later_ref, input_ref, scale_ref, *, factor):
+def gather_kernel(mine_ref, got1, got3, got2, later_ref, token_ref, input_ref, scale_ref, *, factor):
     total = mine_ref[...] + (got1[...] + got3[...]) + got2[...]
     size = input_ref.shape[0]
     input_ref[...] = total[:size].astype(BF16)
@@ -168,44 +168,26 @@
             target_ref[offset : offset + tokens, :] = source_ref[:, k * part : (k + 1) * part]
 
 
-def pair_kernel(*refs):
-    got, swap = refs[:2], refs[2:4]
-    wg_ref, wu_ref, wd_ref, g_ref, u_ref, h_ref, xp_ref, dyp_ref, xs, dys = refs[4:]
-    merge(got, swap, xs, dys)
-    take_part(xs, xp_ref, 0)
-    take_part(dys, dyp_ref, 0)
-    g, u, h = forward(xs[...], dys[...], wg_ref[...], wu_ref[...], wd_ref[...])
-    g_ref[...] = g
-    u_ref[...] = u
-    h_ref[...] = h
-
-
-def last_kernel(
-    scale0, scale1, scale2, scale3, x_ref, dy_ref, g_ref, u_ref, h_ref, g12_ref, u12_ref, h12_ref, xp_ref, dyp_ref,
-    got0, got1, swap0, swap1, wg_ref, wu_ref, wd_ref, *refs,
+def group_kernel(
+    scale0, scale1, scale2, scale3, x_ref, dy_ref, g_ref, u_ref, h_ref, got0, got1, got2, got3,
+    swap0, swap1, swap2, swap3, wg_ref, wu_ref, wd_ref, *refs,
 ):
     out_refs = refs[: 2 * NZ]
     xs, dys, x_part, dy_part, blocks = refs[2 * NZ :]
     tokens, width = x_ref.shape
     part = width // NY
-    merge((got0, got1), (swap0, swap1), xs, dys)
+    merge((got0, got1, got2, got3), (swap0, swap1, swap2, swap3), xs, dys)
     take_part(x_ref, x_part, 0)
     take_part(dy_ref, dy_part, 0)
-    take_part(xs, x_part, 3 * tokens)
-    take_part(dys, dy_part, 3 * tokens)
-    x_part[tokens : 3 * tokens, :] = xp_ref[...]
-    dy_part[tokens : 3 * tokens, :] = dyp_ref[...]
-    last = forward(xs[...], dys[...], wg_ref[...], wu_ref[...], wd_ref[...])
+    take_part(xs, x_part, tokens)
+    take_part(dys, dy_part, tokens)
+    others = forward(xs[...], dys[...], wg_ref[...], wu_ref[...], wd_ref[...])
     rows = part // NZ
     half = blocks.shape[2]
-    for m, (left, mine, pair, other) in enumerate(
-        (
-            (x_part, g_ref, g12_ref, last[0]),
-            (x_part, u_ref, u12_ref, last[1]),
-            (dy_part, h_ref, h12_ref, last[2]),
-        )
+    for m, (left, mine, other) in enumerate(
+        ((x_part, g_ref, others[0]), (x_part, u_ref, others[1]), (dy_part, h_ref, others[2]))
     ):
-        pieces = (mine[...], pair[:tokens], pair[tokens:], other)
+        pieces = [mine[...]] + [other[e * tokens : (e + 1) * tokens] for e in range(NY - 1)]
         scaled = [
             (piece.astype(F32) * scale[0:1, 0:1]).astype(BF16)
             for piece, scale in zip(pieces, (scale0, scale1, scale2, scale3))
@@ -290,15 +272,6 @@
         spread_kernel, "input_spread", [one] * 4, [pltpu.VMEM(group.shape, F32)], 0, 4,
         keep, shift(give, "core", 1),
     )
-    rest = [shift(a, "x", k) for a, k in zip(rest, (1, 3, 2))]
-    input_grad, scale = call(
-        functools.partial(gather_kernel, factor=math.sqrt(width * ff * NX * NC / (NY * NZ))),
-        "input_sum", [shape(slice_rows, width, dtype=BF16), shape(8, 128)], [], 0, 2,
-        first, *rest, later_norms,
-        spaces=[(4, pltpu.SMEM)],
-    )
-    scales = [scale] + [shift(scale, "y", k) for k in (1, 3, 2)]
-
     half = shape(tokens // 2, width)
     any_space = pl.BlockSpec(memory_space=pl.ANY)
     vmem_space = pl.BlockSpec(memory_space=pltpu.VMEM)
@@ -312,19 +285,24 @@
         name="forward",
     )(up, down, give)
     far = [shift(low, "y", 1), shift(high, "y", -1)]
-    near = after(rest[2], up, down)
+    rest = [shift(a, "x", k) for a, k in zip(rest, (1, 3, 2))]
+    input_grad, scale = call(
+        functools.partial(gather_kernel, factor=math.sqrt(width * ff * NX * NC / (NY * NZ))),
+        "input_sum", [shape(slice_rows, width, dtype=BF16), shape(8, 128)], [], 0, 2,
+        first, *rest, later_norms, low,
+        spaces=[(4, pltpu.SMEM), (5, pl.ANY)],
+    )
+    scales = [scale] + [shift(scale, "y", k) for k in (1, 3, 2)]
+
+    near = after(scales[1], up, down)
     near_swap = [shift(a, "core", 1) for a in near]
+    far = after(scales[3], *far)
     far_swap = [shift(a, "core", 1) for a in far]
-    both = [shape(2 * tokens, ff, dtype=BF16)] * 3 + [shape(2 * tokens, part, dtype=BF16)] * 2
-    pair_back = call(
-        pair_kernel, "pair_examples", both, [pltpu.VMEM((2 * tokens, width), BF16)] * 2, 6, 16,
-        *near, *near_swap, *weights,
-    )
     blocks = call(
-        last_kernel, "group_gradients", [shape(half_rows, ff)] * (2 * NZ),
-        [pltpu.VMEM((tokens, width), BF16)] * 2 + [pltpu.VMEM((NY * tokens, part), BF16)] * 2
-        + [pltpu.VMEM((NZ, 2, half_rows, ff), F32)], 6, 20,
-        *scales, inputs, out_grad, *own_back, *pair_back, *far, *far_swap, *weights,
+        group_kernel, "group_gradients", [shape(half_rows, ff)] * (2 * NZ),
+        [pltpu.VMEM(((NY - 1) * tokens, width), BF16)] * 2 + [pltpu.VMEM((NY * tokens, part), BF16)] * 2
+        + [pltpu.VMEM((NZ, 2, half_rows, ff), F32)], 12, 24,
+        *scales, inputs, out_grad, *own_back, *near, *far, *near_swap, *far_swap, *weights,
     )
     plan = ((0, 1, 4), (1, -1, 4), (1, 1, 3), (0, -1, 3))
     held = [blocks[2 * (d * n % NZ) + i] for i, d, n in plan]

time: 87.8 us -> 84.1 us (0.958); the launches traced: 87.6 us -> 82.6 us
  Pallas kernels: 16.1 us -> 13 us
  starting transfers between devices: 39.7 us -> 37.6 us
    pallas_call x17 -> x16, Pallas kernels: 16.1 us -> 12.9 us  [call(): pl.pallas_call(kernel, out_shape=outs, in_specs=[pl.BlockSpec(memory_spac...]
    ppermute x29, starting transfers between devices: 39.7 us -> 37.6 us  [shift(): lax.ppermute(array, axis, [(i, (i + step) % size) for i in range(size)])]
  transfers between devices with their start and end apart: 29 -> 29, of which waited for: 12 -> 13; matrix products, arithmetic and copies ran while one was open for 0% -> 0% of each run, Pallas kernels for 11% -> 8%
where the time goes in v4:
time: 84.1 us; the launch traced here: 82.6 us
  starting transfers between devices  37.6 us (45%)
  waiting for transfers between devices  28.6 us (34%)
  Pallas kernels  13 us (15%)
  local copies, waits for them, and re-layouts  1.92 us (2%)
  between operations  1.48 us (2%)
    ppermute x29, starting transfers between devices, shift(): lax.ppermute(array, axis, [(i, (i + step) % size) for i in range(size)])  37.6 us
    ppermute x29, waiting for transfers between devices, shift(): lax.ppermute(array, axis, [(i, (i + step) % size) for i in range(size)])  28.6 us
    pallas_call x16, Pallas kernels, call(): pl.pallas_call(kernel, out_shape=outs, in_specs=[pl.BlockSpec(memory_spac...  12.9 us
    unnamed x6, local copies, waits for them, and re-layouts  1.92 us
  transfers between devices with their start and end apart: 29, of which 13 were waited for; matrix products, arithmetic and copies ran while one was open for 0% of the time, Pallas kernels for 8%

profile of v4, /device:TPU:96, one launch (start us, length us, event | category | flops | bytes accessed | tf_op | source)
XLA Modules:
  0.0 82.6 jit_solution(14824000191417290951)
XLA Ops:
  0.6 1.0 %copy-done = bf16[128,1152]{1,0:T(8,128)(2,1)S(1)} copy-done((bf16[128,1152]{1,0:T(8,128)(2,1)S(1)}, bf16[128,1152]{1,0:T(8,128)(2,1)}, u32[]{:S(2)}) %copy-start) | copy-done | bytes 294936
  1.6 1.0 %copy-done.1 = bf16[128,1152]{1,0:T(8,128)(2,1)S(1)} copy-done((bf16[128,1152]{1,0:T(8,128)(2,1)S(1)}, bf16[128,1152]{1,0:T(8,128)(2,1)}, u32[]{:S(2)}) %copy-start.1) | copy-done | bytes 294936
  2.6 0.1 prepare.1
  2.6 3.1 %collective-permute-start.5 = (f32[128,1152]{1,0:T(8,128)S(1)}, f32[128,1152]{1,0:T(8,128)S(1)}, u32[]{:S(2)}, u32[]{:S(2)}) collective-permute-start(f32[128,1152]{1,0:T(8,128)S(1)} %get-tuple-element.56), channel_id=1, source_target_pairs={{0,192},{64,0},{128,64},{192,128},{1,193},{65,1},{129,65},{193,129... | collective-permute-start | bytes 1769480 | tf_op jit(solution)/shard_map/ppermute | solution.py:31
  5.7 0.0 collective-permute-start.4
  5.7 6.1 %own_example.1 = (bf16[128,864]{1,0:T(8,128)(2,1)S(1)}, bf16[128,864]{1,0:T(8,128)(2,1)S(1)}, bf16[128,864]{1,0:T(8,128)(2,1)S(1)}, f32[5,16,1152]{2,1,0:T(8,128...) custom-call(bf16[128,1152]{1,0:T(8,128)(2,1)S(1)} %get-tuple-element, ...), custom_call_target="tpu_custom_call" | custom-call | tf_op jit(solution)/shard_map/own_example/pallas_call | solution.py:241
  11.9 0.1 collective-permute-start
  12.0 1.7 %collective-permute-done.got_ref = f32[5,16,1152]{2,1,0:T(8,128)S(1)} collective-permute-done((f32[5,16,1152]{2,1,0:T(8,128)S(1)}, f32[5,16,1152]{2,1,0:T(8,128)S(1)}, u32[]{:S(2)}, u32[]{:S(2)}) %collective-permute-start) | collective-permute-done | bytes 368672 | tf_op jit(solution)/shard_map/ppermute | solution.py:31
  13.7 0.1 input_spread.1
  13.7 1.6 %collective-permute-start.1 = (f32[24,1152]{1,0:T(8,128)S(1)}, f32[24,1152]{1,0:T(8,128)S(1)}, u32[]{:S(2)}, u32[]{:S(2)}) collective-permute-start(f32[24,1152]{1,0:T(8,128)S(1)} %get-tuple-element.53), channel_id=1, source_target_pairs={{0,2},{2,4},{4,6},{6,0},{1,3},{3,5},{5,7},{7,1},{8,10},{10,12},{12... | collective-permute-start | bytes 331784 | tf_op jit(solution)/shard_map/ppermute | solution.py:31
  15.3 1.7 %collective-permute-start.2 = (f32[24,1152]{1,0:T(8,128)S(1)}, f32[24,1152]{1,0:T(8,128)S(1)}, u32[]{:S(2)}, u32[]{:S(2)}) collective-permute-start(f32[24,1152]{1,0:T(8,128)S(1)} %get-tuple-element.54), channel_id=1, source_target_pairs={{0,6},{2,0},{4,2},{6,4},{1,7},{3,1},{5,3},{7,5},{8,14},{10,8},{12,... | collective-permute-start | bytes 331784 | tf_op jit(solution)/shard_map/ppermute | solution.py:31
  17.0 1.8 %collective-permute-start.3 = (f32[24,1152]{1,0:T(8,128)S(1)}, f32[24,1152]{1,0:T(8,128)S(1)}, u32[]{:S(2)}, u32[]{:S(2)}) collective-permute-start(f32[24,1152]{1,0:T(8,128)S(1)} %get-tuple-element.55), channel_id=1, source_target_pairs={{0,4},{2,6},{4,0},{6,2},{1,5},{3,7},{5,1},{7,3},{8,12},{10,14},{12... | collective-permute-start | bytes 331784 | tf_op jit(solution)/shard_map/ppermute | solution.py:31
  19.5 0.0 collective-permute-done.5.down_ref
  19.5 2.2 %collective-permute-done.4.up_ref = f32[128,1152]{1,0:T(8,128)S(1)} collective-permute-done((f32[128,1152]{1,0:T(8,128)S(1)}, f32[128,1152]{1,0:T(8,128)S(1)}, u32[]{:S(2)}, u32[]{:S(2)}) %collective-permute-start.4) | collective-permute-done | bytes 589856 | tf_op jit(solution)/shard_map/ppermute | solution.py:31
  21.8 0.0 collective-permute-done.1.got1
  21.8 0.0 collective-permute-done.2.got3
  21.8 1.7 %collective-permute-done.3.got2 = f32[24,1152]{1,0:T(8,128)S(1)} collective-permute-done((f32[24,1152]{1,0:T(8,128)S(1)}, f32[24,1152]{1,0:T(8,128)S(1)}, u32[]{:S(2)}, u32[]{:S(2)}) %collective-permute-start.3) | collective-permute-done | bytes 110624 | tf_op jit(solution)/shard_map/ppermute | solution.py:31
  23.5 0.6 input_sum.1
  24.1 0.6 collective-permute-start.6
  24.7 1.6 %collective-permute-start.9 = (f32[64,1152]{1,0:T(8,128)S(1)}, f32[64,1152]{1,0:T(8,128)S(1)}, u32[]{:S(2)}, u32[]{:S(2)}) collective-permute-start(f32[64,1152]{1,0:T(8,128)S(1)} %get-tuple-element.57.token_ref), channel_id=1, source_target_pairs={{0,64},{64,128},{128,192},{192,0},{1,65},{65,129},{129,193},{193,1... | collective-permute-start | bytes 884744 | tf_op jit(solution)/shard_map/ppermute | solution.py:31
  26.3 1.7 %collective-permute-start.10 = (f32[64,1152]{1,0:T(8,128)S(1)}, f32[64,1152]{1,0:T(8,128)S(1)}, u32[]{:S(2)}, u32[]{:S(2)}) collective-permute-start(f32[64,1152]{1,0:T(8,128)S(1)} %get-tuple-element.67), channel_id=1, source_target_pairs={{0,192},{64,0},{128,64},{192,128},{1,193},{65,1},{129,65},{193,129... | collective-permute-start | bytes 884744 | tf_op jit(solution)/shard_map/ppermute | solution.py:31
  27.9 1.1 %collective-permute-done.6.refs_2_.scale1 = f32[8,128]{1,0:T(8,128)S(1)} collective-permute-done((f32[8,128]{1,0:T(8,128)S(1)}, f32[8,128]{1,0:T(8,128)S(1)}, u32[]{:S(2)}, u32[]{:S(2)}) %collective-permute-start.6) | collective-permute-done | bytes 4128 | tf_op jit(solution)/shard_map/ppermute | solution.py:31
  29.0 0.0 collective-permute-start.11
  29.0 0.5 collective-permute-start.12
  29.6 1.8 %collective-permute-start.8 = (f32[8,128]{1,0:T(8,128)S(1)}, f32[8,128]{1,0:T(8,128)S(1)}, u32[]{:S(2)}, u32[]{:S(2)}) collective-permute-start(f32[8,128]{1,0:T(8,128)S(1)} %get-tuple-element.59.scale0), channel_id=1, source_target_pairs={{0,128},{64,192},{128,0},{192,64},{1,129},{65,193},{129,1},{193,65... | collective-permute-start | bytes 12296 | tf_op jit(solution)/shard_map/ppermute | solution.py:31
  31.4 3.6 %collective-permute-done.8.refs_2_.scale3 = f32[8,128]{1,0:T(8,128)S(1)} collective-permute-done((f32[8,128]{1,0:T(8,128)S(1)}, f32[8,128]{1,0:T(8,128)S(1)}, u32[]{:S(2)}, u32[]{:S(2)}) %collective-permute-start.8) | collective-permute-done | bytes 4128 | tf_op jit(solution)/shard_map/ppermute | solution.py:31
  34.9 0.0 collective-permute-done.10.refs_1_
  34.9 0.0 collective-permute-done.9.refs_0_
  34.9 0.1 collective-permute-start.13
  35.0 0.5 collective-permute-start.14
  35.5 2.3 %collective-permute-start.7 = (f32[8,128]{1,0:T(8,128)S(1)}, f32[8,128]{1,0:T(8,128)S(1)}, u32[]{:S(2)}, u32[]{:S(2)}) collective-permute-start(f32[8,128]{1,0:T(8,128)S(1)} %get-tuple-element.59.scale0), channel_id=1, source_target_pairs={{0,192},{64,0},{128,64},{192,128},{1,193},{65,1},{129,65},{193,129... | collective-permute-start | bytes 12296 | tf_op jit(solution)/shard_map/ppermute | solution.py:31
  37.8 1.3 %collective-permute-done.7.scale2 = f32[8,128]{1,0:T(8,128)S(1)} collective-permute-done((f32[8,128]{1,0:T(8,128)S(1)}, f32[8,128]{1,0:T(8,128)S(1)}, u32[]{:S(2)}, u32[]{:S(2)}) %collective-permute-start.7) | collective-permute-done | bytes 4128 | tf_op jit(solution)/shard_map/ppermute | solution.py:31
  39.1 0.0 collective-permute-done.13.swap2
  39.1 0.0 collective-permute-done.14.swap3
  39.1 0.0 collective-permute-done.11.swap0
  39.2 0.0 collective-permute-done.12.swap1
  39.2 4.9 %group_gradients.1 = (f32[56,864]{1,0:T(8,128)S(1)}, f32[56,864]{1,0:T(8,128)S(1)}, f32[56,864]{1,0:T(8,128)S(1)}, f32[56,864]{1,0:T(8,128)S(1)}, f32[56,864]{1,...) custom-call(f32[8,128]{1,0:T(8,128)S(1)} %get-tuple-element.59.scale, ...), custom_call_target="tpu_custom_call" | custom-call | flops 6115295232 | bytes 10780672 | tf_op jit(solution)/shard_map/group_gradients/pallas_call | solution.py:241
  44.1 3.2 %collective-permute-start.15 = (f32[56,864]{1,0:T(8,128)S(1)}, f32[56,864]{1,0:T(8,128)S(1)}, u32[]{:S(2)}, u32[]{:S(2)}) collective-permute-start(f32[56,864]{1,0:T(8,128)S(1)} %get-tuple-element.74), channel_id=1, source_target_pairs={{0,8},{8,16},{16,24},{24,32},{32,40},{40,48},{48,56},{56,0},{1,9},... | collective-permute-start | bytes 580616 | tf_op jit(solution)/shard_map/ppermute | solution.py:31
  47.3 0.0 collective-permute-start.22
  47.3 0.0 collective-permute-start.19
  47.3 3.3 %collective-permute-start.26 = (f32[56,864]{1,0:T(8,128)S(1)}, f32[56,864]{1,0:T(8,128)S(1)}, u32[]{:S(2)}, u32[]{:S(2)}) collective-permute-start(f32[56,864]{1,0:T(8,128)S(1)} %get-tuple-element.86), channel_id=1, source_target_pairs={{0,8},{8,16},{16,24},{24,32},{32,40},{40,48},{48,56},{56,0},{1,9},... | collective-permute-start | bytes 580616 | tf_op jit(solution)/shard_map/ppermute | solution.py:31
  50.6 2.1 %collective-permute-done.15.a_ref = f32[56,864]{1,0:T(8,128)S(1)} collective-permute-done((f32[56,864]{1,0:T(8,128)S(1)}, f32[56,864]{1,0:T(8,128)S(1)}, u32[]{:S(2)}, u32[]{:S(2)}) %collective-permute-start.15) | collective-permute-done | bytes 193568 | tf_op jit(solution)/shard_map/ppermute | solution.py:31
  52.7 3.8 %collective-permute-start.16 = (f32[56,864]{1,0:T(8,128)S(1)}, f32[56,864]{1,0:T(8,128)S(1)}, u32[]{:S(2)}, u32[]{:S(2)}) collective-permute-start(f32[56,864]{1,0:T(8,128)S(1)} %add_block.10), channel_id=1, source_target_pairs={{0,8},{8,16},{16,24},{24,32},{32,40},{40,48},{48,56},{56,0},{1,9},... | collective-permute-start | bytes 580616 | tf_op jit(solution)/shard_map/ppermute | solution.py:31
  56.5 0.0 collective-permute-done.22.a_ref
  56.5 0.1 collective-permute-start.23
  56.6 3.9 %collective-permute-done.19.a_ref = f32[56,864]{1,0:T(8,128)S(1)} collective-permute-done((f32[56,864]{1,0:T(8,128)S(1)}, f32[56,864]{1,0:T(8,128)S(1)}, u32[]{:S(2)}, u32[]{:S(2)}) %collective-permute-start.19) | collective-permute-done | bytes 193568 | tf_op jit(solution)/shard_map/ppermute | solution.py:31
  60.6 0.1 collective-permute-start.20
  60.7 0.0 collective-permute-done.26.a_ref
  60.7 3.5 %collective-permute-start.27 = (f32[56,864]{1,0:T(8,128)S(1)}, f32[56,864]{1,0:T(8,128)S(1)}, u32[]{:S(2)}, u32[]{:S(2)}) collective-permute-start(f32[56,864]{1,0:T(8,128)S(1)} %add_block.18), channel_id=1, source_target_pairs={{0,8},{8,16},{16,24},{24,32},{32,40},{40,48},{48,56},{56,0},{1,9},... | collective-permute-start | bytes 580616 | tf_op jit(solution)/shard_map/ppermute | solution.py:31
  64.3 0.1 collective-permute-start.17
  64.4 1.4 %collective-permute-done.23.a_ref = f32[56,864]{1,0:T(8,128)S(1)} collective-permute-done((f32[56,864]{1,0:T(8,128)S(1)}, f32[56,864]{1,0:T(8,128)S(1)}, u32[]{:S(2)}, u32[]{:S(2)}) %collective-permute-start.23) | collective-permute-done | bytes 193568 | tf_op jit(solution)/shard_map/ppermute | solution.py:31
  65.8 0.7 collective-permute-start.24
  66.5 3.6 %collective-permute-done.20.a_ref = f32[56,864]{1,0:T(8,128)S(1)} collective-permute-done((f32[56,864]{1,0:T(8,128)S(1)}, f32[56,864]{1,0:T(8,128)S(1)}, u32[]{:S(2)}, u32[]{:S(2)}) %collective-permute-start.20) | collective-permute-done | bytes 193568 | tf_op jit(solution)/shard_map/ppermute | solution.py:31
  70.1 0.1 collective-permute-start.21
  70.2 0.0 collective-permute-done.27.a_ref
  70.2 3.3 %collective-permute-start.28 = (f32[56,864]{1,0:T(8,128)S(1)}, f32[56,864]{1,0:T(8,128)S(1)}, u32[]{:S(2)}, u32[]{:S(2)}) collective-permute-start(f32[56,864]{1,0:T(8,128)S(1)} %add_block.19), channel_id=1, source_target_pairs={{0,8},{8,16},{16,24},{24,32},{32,40},{40,48},{48,56},{56,0},{1,9},... | collective-permute-start | bytes 580616 | tf_op jit(solution)/shard_map/ppermute | solution.py:31
  73.5 0.0 collective-permute-done.17.a_ref
  73.5 1.2 %collective-permute-start.18 = (f32[56,864]{1,0:T(8,128)S(1)}, f32[56,864]{1,0:T(8,128)S(1)}, u32[]{:S(2)}, u32[]{:S(2)}) collective-permute-start(f32[56,864]{1,0:T(8,128)S(1)} %add_block.12), channel_id=1, source_target_pairs={{0,8},{8,16},{16,24},{24,32},{32,40},{40,48},{48,56},{56,0},{1,9},... | collective-permute-start | bytes 580616 | tf_op jit(solution)/shard_map/ppermute | solution.py:31
  74.8 1.0 %collective-permute-start.25 = (f32[56,864]{1,0:T(8,128)S(1)}, f32[56,864]{1,0:T(8,128)S(1)}, u32[]{:S(2)}, u32[]{:S(2)}) collective-permute-start(f32[56,864]{1,0:T(8,128)S(1)} %add_block.17), channel_id=1, source_target_pairs={{0,56},{8,0},{16,8},{24,16},{32,24},{40,32},{48,40},{56,48},{1,57}... | collective-permute-start | bytes 580616 | tf_op jit(solution)/shard_map/ppermute | solution.py:31
  75.7 2.5 %collective-permute-done.21.top2 = f32[56,864]{1,0:T(8,128)S(1)} collective-permute-done((f32[56,864]{1,0:T(8,128)S(1)}, f32[56,864]{1,0:T(8,128)S(1)}, u32[]{:S(2)}, u32[]{:S(2)}) %collective-permute-start.21) | collective-permute-done | bytes 193568 | tf_op jit(solution)/shard_map/ppermute | solution.py:31
  78.2 0.0 collective-permute-done.28.low2
  78.2 1.1 %collective-permute-done.18.top1 = f32[56,864]{1,0:T(8,128)S(1)} collective-permute-done((f32[56,864]{1,0:T(8,128)S(1)}, f32[56,864]{1,0:T(8,128)S(1)}, u32[]{:S(2)}, u32[]{:S(2)}) %collective-permute-start.18) | collective-permute-done | bytes 193568 | tf_op jit(solution)/shard_map/ppermute | solution.py:31
  79.3 2.4 %collective-permute-done.25.low1 = f32[56,864]{1,0:T(8,128)S(1)} collective-permute-done((f32[56,864]{1,0:T(8,128)S(1)}, f32[56,864]{1,0:T(8,128)S(1)}, u32[]{:S(2)}, u32[]{:S(2)}) %collective-permute-start.25) | collective-permute-done | bytes 193568 | tf_op jit(solution)/shard_map/ppermute | solution.py:31
  81.8 0.8 %finish.1 = (f32[36,864]{1,0:T(8,128)}, f32[36,864]{1,0:T(8,128)}, f32[36,864]{1,0:T(8,128)}) custom-call(f32[56,864]{1,0:T(8,128)S(1)} %get-tuple-element.73.top0, f32[56,864]{1,0:T(8,128)S(1)} %collective-permute-done.18.top1, f32[56,864]{1,0:T(8,128)S(1)} %collective-permute-done.21.top2, f32[56,864]{1,0:T(8,128)S(1)} %get-tuple-element.81.low0, ...), custom_call_target="tpu_custom_call" | custom-call | tf_op jit(solution)/shard_map/finish/pallas_call | solution.py:241
  (19 shorter events, 0.3 us)
Async XLA Ops:
  0.6 1.0 %copy-start = (bf16[128,1152]{1,0:T(8,128)(2,1)S(1)}, bf16[128,1152]{1,0:T(8,128)(2,1)}, u32[]{:S(2)}) copy-start(bf16[128,1152]{1,0:T(8,128)(2,1)} %x_ref.1) | copy-start | bytes 884740
  1.6 1.0 %copy-start.1 = (bf16[128,1152]{1,0:T(8,128)(2,1)S(1)}, bf16[128,1152]{1,0:T(8,128)(2,1)}, u32[]{:S(2)}) copy-start(bf16[128,1152]{1,0:T(8,128)(2,1)} %dy_ref.1) | copy-start | bytes 884740
  2.6 16.9 %collective-permute-start.5 = (f32[128,1152]{1,0:T(8,128)S(1)}, f32[128,1152]{1,0:T(8,128)S(1)}, u32[]{:S(2)}, u32[]{:S(2)}) collective-permute-start(f32[128,1152]{1,0:T(8,128)S(1)} %get-tuple-element.56), channel_id=1, source_target_pairs={{0,192},{64,0},{128,64},{192,128},{1,193},{65,1},{129,65},{193,129... | collective-permute-start | bytes 1769480 | tf_op jit(solution)/shard_map/ppermute | solution.py:31
  5.7 16.0 %collective-permute-start.4 = (f32[128,1152]{1,0:T(8,128)S(1)}, f32[128,1152]{1,0:T(8,128)S(1)}, u32[]{:S(2)}, u32[]{:S(2)}) collective-permute-start(f32[128,1152]{1,0:T(8,128)S(1)} %get-tuple-element.56), channel_id=1, source_target_pairs={{0,64},{64,128},{128,192},{192,0},{1,65},{65,129},{129,193},{193,1... | collective-permute-start | bytes 1769480 | tf_op jit(solution)/shard_map/ppermute | solution.py:31
  11.9 1.8 %collective-permute-start = (f32[5,16,1152]{2,1,0:T(8,128)S(1)}, f32[5,16,1152]{2,1,0:T(8,128)S(1)}, u32[]{:S(2)}, u32[]{:S(2)}) collective-permute-start(f32[5,16,1152]{2,1,0:T(8,128)S(1)} %get-tuple-element.51.token_ref), channel_id=1, source_target_pairs={{0,1},{1,0},{2,3},{3,2},{4,5},{5,4},{6,7},{7,6},{8,9},{9,8},{10,11... | collective-permute-start | bytes 1105928 | tf_op jit(solution)/shard_map/ppermute | solution.py:31
  13.7 8.0 %collective-permute-start.1 = (f32[24,1152]{1,0:T(8,128)S(1)}, f32[24,1152]{1,0:T(8,128)S(1)}, u32[]{:S(2)}, u32[]{:S(2)}) collective-permute-start(f32[24,1152]{1,0:T(8,128)S(1)} %get-tuple-element.53), channel_id=1, source_target_pairs={{0,2},{2,4},{4,6},{6,0},{1,3},{3,5},{5,7},{7,1},{8,10},{10,12},{12... | collective-permute-start | bytes 331784 | tf_op jit(solution)/shard_map/ppermute | solution.py:31
  15.3 6.5 %collective-permute-start.2 = (f32[24,1152]{1,0:T(8,128)S(1)}, f32[24,1152]{1,0:T(8,128)S(1)}, u32[]{:S(2)}, u32[]{:S(2)}) collective-permute-start(f32[24,1152]{1,0:T(8,128)S(1)} %get-tuple-element.54), channel_id=1, source_target_pairs={{0,6},{2,0},{4,2},{6,4},{1,7},{3,1},{5,3},{7,5},{8,14},{10,8},{12,... | collective-permute-start | bytes 331784 | tf_op jit(solution)/shard_map/ppermute | solution.py:31
  17.0 6.4 %collective-permute-start.3 = (f32[24,1152]{1,0:T(8,128)S(1)}, f32[24,1152]{1,0:T(8,128)S(1)}, u32[]{:S(2)}, u32[]{:S(2)}) collective-permute-start(f32[24,1152]{1,0:T(8,128)S(1)} %get-tuple-element.55), channel_id=1, source_target_pairs={{0,4},{2,6},{4,0},{6,2},{1,5},{3,7},{5,1},{7,3},{8,12},{10,14},{12... | collective-permute-start | bytes 331784 | tf_op jit(solution)/shard_map/ppermute | solution.py:31
  19.5 19.7 %copy-start.2 = (bf16[864,1152]{1,0:T(8,128)(2,1)S(1)}, bf16[864,1152]{1,0:T(8,128)(2,1)}, u32[]{:S(2)}) copy-start(bf16[864,1152]{1,0:T(8,128)(2,1)} %get-tuple-element.72.wd_ref) | copy-start | bytes 5971972
  24.1 4.9 %collective-permute-start.6 = (f32[8,128]{1,0:T(8,128)S(1)}, f32[8,128]{1,0:T(8,128)S(1)}, u32[]{:S(2)}, u32[]{:S(2)}) collective-permute-start(f32[8,128]{1,0:T(8,128)S(1)} %get-tuple-element.59.scale0), channel_id=1, source_target_pairs={{0,64},{64,128},{128,192},{192,0},{1,65},{65,129},{129,193},{193,1... | collective-permute-start | bytes 12296 | tf_op jit(solution)/shard_map/ppermute | solution.py:31
  24.7 10.2 %collective-permute-start.9 = (f32[64,1152]{1,0:T(8,128)S(1)}, f32[64,1152]{1,0:T(8,128)S(1)}, u32[]{:S(2)}, u32[]{:S(2)}) collective-permute-start(f32[64,1152]{1,0:T(8,128)S(1)} %get-tuple-element.57.token_ref), channel_id=1, source_target_pairs={{0,64},{64,128},{128,192},{192,0},{1,65},{65,129},{129,193},{193,1... | collective-permute-start | bytes 884744 | tf_op jit(solution)/shard_map/ppermute | solution.py:31
  26.3 8.7 %collective-permute-start.10 = (f32[64,1152]{1,0:T(8,128)S(1)}, f32[64,1152]{1,0:T(8,128)S(1)}, u32[]{:S(2)}, u32[]{:S(2)}) collective-permute-start(f32[64,1152]{1,0:T(8,128)S(1)} %get-tuple-element.67), channel_id=1, source_target_pairs={{0,192},{64,0},{128,64},{192,128},{1,193},{65,1},{129,65},{193,129... | collective-permute-start | bytes 884744 | tf_op jit(solution)/shard_map/ppermute | solution.py:31
  29.0 10.1 %collective-permute-start.11 = (f32[128,1152]{1,0:T(8,128)S(1)}, f32[128,1152]{1,0:T(8,128)S(1)}, u32[]{:S(2)}, u32[]{:S(2)}) collective-permute-start(f32[128,1152]{1,0:T(8,128)S(1)} %get-tuple-element.65.got0), channel_id=1, source_target_pairs={{0,1},{1,0},{2,3},{3,2},{4,5},{5,4},{6,7},{7,6},{8,9},{9,8},{10,11... | collective-permute-start | bytes 1769480 | tf_op jit(solution)/shard_map/ppermute | solution.py:31
  29.0 10.1 %collective-permute-start.12 = (f32[128,1152]{1,0:T(8,128)S(1)}, f32[128,1152]{1,0:T(8,128)S(1)}, u32[]{:S(2)}, u32[]{:S(2)}) collective-permute-start(f32[128,1152]{1,0:T(8,128)S(1)} %get-tuple-element.66.got1), channel_id=1, source_target_pairs={{0,1},{1,0},{2,3},{3,2},{4,5},{5,4},{6,7},{7,6},{8,9},{9,8},{10,11... | collective-permute-start | bytes 1769480 | tf_op jit(solution)/shard_map/ppermute | solution.py:31
  29.6 5.4 %collective-permute-start.8 = (f32[8,128]{1,0:T(8,128)S(1)}, f32[8,128]{1,0:T(8,128)S(1)}, u32[]{:S(2)}, u32[]{:S(2)}) collective-permute-start(f32[8,128]{1,0:T(8,128)S(1)} %get-tuple-element.59.scale0), channel_id=1, source_target_pairs={{0,128},{64,192},{128,0},{192,64},{1,129},{65,193},{129,1},{193,65... | collective-permute-start | bytes 12296 | tf_op jit(solution)/shard_map/ppermute | solution.py:31
  34.9 4.2 %collective-permute-start.13 = (f32[64,1152]{1,0:T(8,128)S(1)}, f32[64,1152]{1,0:T(8,128)S(1)}, u32[]{:S(2)}, u32[]{:S(2)}) collective-permute-start(f32[64,1152]{1,0:T(8,128)S(1)} %get-tuple-element.68.got2), channel_id=1, source_target_pairs={{0,1},{1,0},{2,3},{3,2},{4,5},{5,4},{6,7},{7,6},{8,9},{9,8},{10,11... | collective-permute-start | bytes 884744 | tf_op jit(solution)/shard_map/ppermute | solution.py:31
  35.0 4.1 %collective-permute-start.14 = (f32[64,1152]{1,0:T(8,128)S(1)}, f32[64,1152]{1,0:T(8,128)S(1)}, u32[]{:S(2)}, u32[]{:S(2)}) collective-permute-start(f32[64,1152]{1,0:T(8,128)S(1)} %get-tuple-element.69.got3), channel_id=1, source_target_pairs={{0,1},{1,0},{2,3},{3,2},{4,5},{5,4},{6,7},{7,6},{8,9},{9,8},{10,11... | collective-permute-start | bytes 884744 | tf_op jit(solution)/shard_map/ppermute | solution.py:31
  35.5 3.6 %collective-permute-start.7 = (f32[8,128]{1,0:T(8,128)S(1)}, f32[8,128]{1,0:T(8,128)S(1)}, u32[]{:S(2)}, u32[]{:S(2)}) collective-permute-start(f32[8,128]{1,0:T(8,128)S(1)} %get-tuple-element.59.scale0), channel_id=1, source_target_pairs={{0,192},{64,0},{128,64},{192,128},{1,193},{65,1},{129,65},{193,129... | collective-permute-start | bytes 12296 | tf_op jit(solution)/shard_map/ppermute | solution.py:31
  44.1 8.6 %collective-permute-start.15 = (f32[56,864]{1,0:T(8,128)S(1)}, f32[56,864]{1,0:T(8,128)S(1)}, u32[]{:S(2)}, u32[]{:S(2)}) collective-permute-start(f32[56,864]{1,0:T(8,128)S(1)} %get-tuple-element.74), channel_id=1, source_target_pairs={{0,8},{8,16},{16,24},{24,32},{32,40},{40,48},{48,56},{56,0},{1,9},... | collective-permute-start | bytes 580616 | tf_op jit(solution)/shard_map/ppermute | solution.py:31
  47.3 9.2 %collective-permute-start.22 = (f32[56,864]{1,0:T(8,128)S(1)}, f32[56,864]{1,0:T(8,128)S(1)}, u32[]{:S(2)}, u32[]{:S(2)}) collective-permute-start(f32[56,864]{1,0:T(8,128)S(1)} %get-tuple-element.82), channel_id=1, source_target_pairs={{0,56},{8,0},{16,8},{24,16},{32,24},{40,32},{48,40},{56,48},{1,57}... | collective-permute-start | bytes 580616 | tf_op jit(solution)/shard_map/ppermute | solution.py:31
  47.3 13.3 %collective-permute-start.19 = (f32[56,864]{1,0:T(8,128)S(1)}, f32[56,864]{1,0:T(8,128)S(1)}, u32[]{:S(2)}, u32[]{:S(2)}) collective-permute-start(f32[56,864]{1,0:T(8,128)S(1)} %get-tuple-element.78), channel_id=1, source_target_pairs={{0,56},{8,0},{16,8},{24,16},{32,24},{40,32},{48,40},{56,48},{1,57}... | collective-permute-start | bytes 580616 | tf_op jit(solution)/shard_map/ppermute | solution.py:31
  47.3 13.4 %collective-permute-start.26 = (f32[56,864]{1,0:T(8,128)S(1)}, f32[56,864]{1,0:T(8,128)S(1)}, u32[]{:S(2)}, u32[]{:S(2)}) collective-permute-start(f32[56,864]{1,0:T(8,128)S(1)} %get-tuple-element.86), channel_id=1, source_target_pairs={{0,8},{8,16},{16,24},{24,32},{32,40},{40,48},{48,56},{56,0},{1,9},... | collective-permute-start | bytes 580616 | tf_op jit(solution)/shard_map/ppermute | solution.py:31
  52.7 11.5 %collective-permute-start.16 = (f32[56,864]{1,0:T(8,128)S(1)}, f32[56,864]{1,0:T(8,128)S(1)}, u32[]{:S(2)}, u32[]{:S(2)}) collective-permute-start(f32[56,864]{1,0:T(8,128)S(1)} %add_block.10), channel_id=1, source_target_pairs={{0,8},{8,16},{16,24},{24,32},{32,40},{40,48},{48,56},{56,0},{1,9},... | collective-permute-start | bytes 580616 | tf_op jit(solution)/shard_map/ppermute | solution.py:31
  56.5 9.2 %collective-permute-start.23 = (f32[56,864]{1,0:T(8,128)S(1)}, f32[56,864]{1,0:T(8,128)S(1)}, u32[]{:S(2)}, u32[]{:S(2)}) collective-permute-start(f32[56,864]{1,0:T(8,128)S(1)} %add_block.15), channel_id=1, source_target_pairs={{0,56},{8,0},{16,8},{24,16},{32,24},{40,32},{48,40},{56,48},{1,57}... | collective-permute-start | bytes 580616 | tf_op jit(solution)/shard_map/ppermute | solution.py:31
  60.6 9.5 %collective-permute-start.20 = (f32[56,864]{1,0:T(8,128)S(1)}, f32[56,864]{1,0:T(8,128)S(1)}, u32[]{:S(2)}, u32[]{:S(2)}) collective-permute-start(f32[56,864]{1,0:T(8,128)S(1)} %add_block.13), channel_id=1, source_target_pairs={{0,56},{8,0},{16,8},{24,16},{32,24},{40,32},{48,40},{56,48},{1,57}... | collective-permute-start | bytes 580616 | tf_op jit(solution)/shard_map/ppermute | solution.py:31
  60.7 9.4 %collective-permute-start.27 = (f32[56,864]{1,0:T(8,128)S(1)}, f32[56,864]{1,0:T(8,128)S(1)}, u32[]{:S(2)}, u32[]{:S(2)}) collective-permute-start(f32[56,864]{1,0:T(8,128)S(1)} %add_block.18), channel_id=1, source_target_pairs={{0,8},{8,16},{16,24},{24,32},{32,40},{40,48},{48,56},{56,0},{1,9},... | collective-permute-start | bytes 580616 | tf_op jit(solution)/shard_map/ppermute | solution.py:31
  64.3 9.2 %collective-permute-start.17 = (f32[56,864]{1,0:T(8,128)S(1)}, f32[56,864]{1,0:T(8,128)S(1)}, u32[]{:S(2)}, u32[]{:S(2)}) collective-permute-start(f32[56,864]{1,0:T(8,128)S(1)} %add_block.11), channel_id=1, source_target_pairs={{0,8},{8,16},{16,24},{24,32},{32,40},{40,48},{48,56},{56,0},{1,9},... | collective-permute-start | bytes 580616 | tf_op jit(solution)/shard_map/ppermute | solution.py:31
  65.8 9.0 %collective-permute-start.24 = (f32[56,864]{1,0:T(8,128)S(1)}, f32[56,864]{1,0:T(8,128)S(1)}, u32[]{:S(2)}, u32[]{:S(2)}) collective-permute-start(f32[56,864]{1,0:T(8,128)S(1)} %add_block.16), channel_id=1, source_target_pairs={{0,56},{8,0},{16,8},{24,16},{32,24},{40,32},{48,40},{56,48},{1,57}... | collective-permute-start | bytes 580616 | tf_op jit(solution)/shard_map/ppermute | solution.py:31
  70.1 8.1 %collective-permute-start.21 = (f32[56,864]{1,0:T(8,128)S(1)}, f32[56,864]{1,0:T(8,128)S(1)}, u32[]{:S(2)}, u32[]{:S(2)}) collective-permute-start(f32[56,864]{1,0:T(8,128)S(1)} %add_block.14), channel_id=1, source_target_pairs={{0,56},{8,0},{16,8},{24,16},{32,24},{40,32},{48,40},{56,48},{1,57}... | collective-permute-start | bytes 580616 | tf_op jit(solution)/shard_map/ppermute | solution.py:31
  70.2 8.0 %collective-permute-start.28 = (f32[56,864]{1,0:T(8,128)S(1)}, f32[56,864]{1,0:T(8,128)S(1)}, u32[]{:S(2)}, u32[]{:S(2)}) collective-permute-start(f32[56,864]{1,0:T(8,128)S(1)} %add_block.19), channel_id=1, source_target_pairs={{0,8},{8,16},{16,24},{24,32},{32,40},{40,48},{48,56},{56,0},{1,9},... | collective-permute-start | bytes 580616 | tf_op jit(solution)/shard_map/ppermute | solution.py:31
  73.5 5.8 %collective-permute-start.18 = (f32[56,864]{1,0:T(8,128)S(1)}, f32[56,864]{1,0:T(8,128)S(1)}, u32[]{:S(2)}, u32[]{:S(2)}) collective-permute-start(f32[56,864]{1,0:T(8,128)S(1)} %add_block.12), channel_id=1, source_target_pairs={{0,8},{8,16},{16,24},{24,32},{32,40},{40,48},{48,56},{56,0},{1,9},... | collective-permute-start | bytes 580616 | tf_op jit(solution)/shard_map/ppermute | solution.py:31
  74.8 7.0 %collective-permute-start.25 = (f32[56,864]{1,0:T(8,128)S(1)}, f32[56,864]{1,0:T(8,128)S(1)}, u32[]{:S(2)}, u32[]{:S(2)}) collective-permute-start(f32[56,864]{1,0:T(8,128)S(1)} %add_block.17), channel_id=1, source_target_pairs={{0,56},{8,0},{16,8},{24,16},{32,24},{40,32},{48,40},{56,48},{1,57}... | collective-permute-start | bytes 580616 | tf_op jit(solution)/shard_map/ppermute | solution.py:31
